TPU v7x, 256 devices: a whole 4x4x8 slice. The times are simulated.
256 devices in a mesh: seq: 128 (over z, y, x_lo, core), head: 2 (over x_hi).
Axes of the slice: x: 4 (x_hi: 2, x_lo: 2; x = x_hi * 2 + x_lo), y: 4, z: 8, core: 2. Of those that a mesh axis runs over, the one named last changes fastest.
Arguments:
- events: bfloat16 [16, 32768, 512], P(None, ('seq', 'head')), may hold values from -6 to 6
- global_tokens: bfloat16 [16, 128, 512], P(None, 'seq'), may hold values from -6 to 6
- lengths: int32 [16], replicated, may hold values from 8 to 32768, as said below
- inner_qkv: bfloat16 [512, 1536], replicated, may hold values from -0.26516504 to 0.26516504
- inner_out: bfloat16 [512, 512], replicated, may hold values from -0.25 to 0.25
- merge_gain: float32 [512], replicated, may hold values from 0.25 to 1.75
- global_gain: float32 [512], replicated, may hold values from 0.25 to 1.75
- mixed_qkv: bfloat16 [512, 1536], replicated, may hold values from -0.26516504 to 0.26516504
- mixed_out: bfloat16 [512, 512], replicated, may hold values from -1.5 to 1.5
Outputs:
- merged_out: bfloat16 [16, 4096, 512], P(None, ('seq', 'head'))
- global_heads: bfloat16 [128, 2, 4096], P('seq', 'head')
Inputs may be any that keep to these rules, and one draw needn't show every extreme that they name: `lengths`: each length is a multiple of 8; some user has the full 32768 events.
All inputs are finite; a program needn't handle non-finite values.
Results may differ from a plain program's by a relative error of at most 0.025.
Values may be sent and summed in bfloat16 or wider, within the bound.
No kernel may reach another device: no remote copies, remote signals or barrier semaphores. Data moves between devices by JAX's collectives and lax.ppermute only.
A program may use at most 128 MiB of HBM per device.

v0:
```python
import jax
import jax.numpy as jnp
from jax import lax
from jax.sharding import PartitionSpec as P


def softmax_last(scores):
    top = jnp.max(scores, axis=-1, keepdims=True)
    expd = jnp.exp(scores - top)
    return expd / jnp.sum(expd, axis=-1, keepdims=True)


def norm_rows(values, gain):
    wide = values.astype(jnp.float32)
    scale = lax.rsqrt(jnp.mean(wide * wide, axis=-1, keepdims=True) + 1e-06)
    return (wide * scale * gain).astype(jnp.bfloat16)


def inner_merge(events, inner_qkv, inner_out):
    users, span, width = events.shape
    groups = span // 8
    head_dim = width // 8
    flat = jnp.dot(
        events.reshape(users * span, width), inner_qkv, preferred_element_type=jnp.float32
    ).astype(jnp.bfloat16)
    flat = flat.reshape(users, groups, 8, 3, 8, head_dim)
    scores = jnp.einsum(
        "ugqhd,ugkhd->ughqk", flat[:, :, :, 0], flat[:, :, :, 1], preferred_element_type=jnp.float32
    )
    scores = scores / jnp.sqrt(jnp.float32(head_dim))
    pooled_w = jnp.mean(softmax_last(scores), axis=3).astype(jnp.bfloat16)
    pooled = jnp.einsum(
        "ughk,ugkhd->ughd", pooled_w, flat[:, :, :, 2], preferred_element_type=jnp.float32
    )
    pooled = pooled.astype(jnp.bfloat16).reshape(users * groups, width)
    mean_events = jnp.mean(events.reshape(users * groups, 8, width).astype(jnp.float32), axis=1)
    merged = mean_events + jnp.dot(pooled, inner_out, preferred_element_type=jnp.float32)
    return merged.astype(jnp.bfloat16).reshape(users, groups, width)


def attend_rows(queries, keys, values, allowed):
    scale = 1.0 / jnp.sqrt(jnp.float32(queries.shape[1]))
    scores = jnp.einsum("qd,kd->qk", queries, keys, preferred_element_type=jnp.float32) * scale
    scores = jnp.where(allowed, scores, jnp.float32(-1e30))
    weights = softmax_last(scores).astype(jnp.bfloat16)
    return jnp.dot(weights, values, preferred_element_type=jnp.float32).astype(jnp.bfloat16)


def pair_attention(merged_qkv, global_qkv, valid):
    count = merged_qkv.shape[0]
    glob = global_qkv.shape[0]
    head_dim = merged_qkv.shape[1] // 3
    keys = jnp.concatenate(
        [global_qkv[:, head_dim : 2 * head_dim], merged_qkv[:, head_dim : 2 * head_dim]], axis=0
    )
    values = jnp.concatenate([global_qkv[:, 2 * head_dim :], merged_qkv[:, 2 * head_dim :]], axis=0)
    columns = jnp.arange(glob + count, dtype=jnp.int32) - glob
    key_live = columns < valid
    glob_out = attend_rows(global_qkv[:, :head_dim], keys, values, key_live[None, :])
    block = min(512, count)
    queries = merged_qkv[:, :head_dim]

    def one_block(start):
        rows = lax.dynamic_slice_in_dim(queries, start, block, 0)
        position = start + jnp.arange(block, dtype=jnp.int32)
        allowed = key_live[None, :] & (columns[None, :] <= position[:, None])
        return attend_rows(rows, keys, values, allowed)

    starts = jnp.arange(count // block, dtype=jnp.int32) * block
    merged_att = lax.map(one_block, starts).reshape(count, head_dim)
    return (merged_att, glob_out)


def per_device(
    events,
    global_tokens,
    lengths,
    inner_qkv,
    inner_out,
    merge_gain,
    global_gain,
    mixed_qkv,
    mixed_out,
):
    users, span, width = events.shape
    groups = span // 8
    head_dim = width // 16
    merged = inner_merge(events, inner_qkv, inner_out)
    normed = norm_rows(merged, merge_gain)
    qkv = jnp.dot(
        normed.reshape(users * groups, width), mixed_qkv, preferred_element_type=jnp.float32
    ).astype(jnp.bfloat16)
    outgoing = (
        qkv.reshape(users, groups, 3, 8, 2, head_dim)
        .transpose(4, 0, 3, 1, 2, 5)
        .reshape(2, users * 8, groups, 3 * head_dim)
    )
    seq_count = lax.axis_size("seq")
    pair_count = users * 8 // seq_count
    seq_index = lax.axis_index("seq")
    parity = lax.axis_index("head")
    pair_ids = seq_index * pair_count + jnp.arange(pair_count, dtype=jnp.int32)
    valid = jnp.take(lengths, pair_ids // 8) // 8
    w_half = lax.dynamic_index_in_dim(
        mixed_qkv.reshape(width, 3, 8, 2, head_dim), parity, 3, keepdims=False
    )
    w_pairs = (
        jnp.take(w_half, pair_ids % 8, axis=2)
        .transpose(2, 0, 1, 3)
        .reshape(pair_count, width, 3 * head_dim)
    )
    pair_users = pair_ids // 8
    chosen = norm_rows(
        jnp.take(lax.all_gather(global_tokens, "seq", axis=1, tiled=True), pair_users, axis=0),
        global_gain,
    )
    global_qkv = jnp.einsum(
        "pcd,pde->pce", chosen, w_pairs, preferred_element_type=jnp.float32
    ).astype(jnp.bfloat16)
    arrived = lax.all_to_all(
        lax.all_to_all(outgoing, "head", split_axis=0, concat_axis=2, tiled=True),
        "seq",
        split_axis=1,
        concat_axis=2,
        tiled=True,
    )
    arrived = arrived.reshape(pair_count, -1, 3 * head_dim)
    att_m, att_g = lax.map(
        lambda item: pair_attention(item[0], item[1], item[2]), (arrived, global_qkv, valid)
    )
    returned = lax.all_to_all(
        lax.all_to_all(att_m[None], "seq", split_axis=2, concat_axis=1, tiled=True),
        "head",
        split_axis=2,
        concat_axis=0,
        tiled=True,
    )
    heads_out = (
        returned.reshape(2, users, 8, groups, head_dim)
        .transpose(1, 3, 2, 0, 4)
        .reshape(users * groups, width)
    )
    merged_out = merged.astype(jnp.float32).reshape(users * groups, width) + jnp.dot(
        heads_out, mixed_out, preferred_element_type=jnp.float32
    )
    merged_out = merged_out.astype(jnp.bfloat16).reshape(users, groups, width)
    global_heads = att_g.reshape(pair_count, 1, -1)
    return (merged_out, global_heads)


def solution(mesh):
    in_specs = (
        P(None, ("seq", "head"), None),
        P(None, "seq", None),
        P(),
        P(),
        P(),
        P(),
        P(),
        P(),
        P(),
    )
    out_specs = (P(None, ("seq", "head"), None), P("seq", "head", None))
    return jax.shard_map(
        per_device, mesh=mesh, in_specs=in_specs, out_specs=out_specs, check_vma=False
    )
```

profile of v0, /device:TPU:1, one launch (start us, length us, event | category | flops | bytes accessed | tf_op | source)
XLA Modules:
  0.0 399.3 jit_solution(1622702099887725899)
XLA Ops:
  8.6 7.0 %convolution_convert_fusion = bf16[2048,1536]{1,0:T(8,128)(2,1)} fusion(bf16[2048,512]{1,0:T(8,128)(2,1)} %bitcast.79, bf16[512,1536]{1,0:T(8,128)(2,1)S(1)} %copy-done), kind=kOutput, calls=%fused_computation.19 | convolution fusion | flops 3224371200 | bytes 9961472 | tf_op jit(solution)/shard_map/dot_general | solution.py:23
  15.6 16.2 %reshape.217 = bf16[16,16,8,3,8,64]{5,4,3,2,1,0:T(8,128)(2,1)} reshape(bf16[2048,1536]{1,0:T(8,128)(2,1)} %convolution_convert_fusion) | data formatting | bytes 12582912 | tf_op jit(solution)/shard_map/reshape | solution.py:26
  31.9 8.1 %fusion.40 = (bf16[16,16,8,1,8,64]{5,4,3,2,1,0:T(8,128)(2,1)S(1)}, bf16[16,16,8,8,64]{4,3,2,1,0:T(8,128)(2,1)}, bf16[16,16,8,1,8,64]{5,4,3,2,1,0:T(8,128)(2,1)S(1)}) fusion(bf16[16,16,8,3,8,64]{5,4,3,2,1,0:T(8,128)(2,1)} %reshape.217), kind=kLoop, calls=%fused_computation.72 | loop fusion | bytes 12582912 | tf_op jit(solution)/shard_map/slice | solution.py:28
  39.9 5.5 %fusion.17 = f32[16,16,8,8,8]{3,4,2,1,0:T(8,128)} fusion(bf16[16,16,8,1,8,64]{5,4,3,2,1,0:T(8,128)(2,1)S(1)} %get-tuple-element.139, bf16[16,16,8,1,8,64]{5,4,3,2,1,0:T(8,128)(2,1)S(1)} %get-tuple-element.137), kind=kOutput, calls=%fused_computation.26 | convolution fusion | flops 16777216 | bytes 4718592 | tf_op jit(solution)/shard_map/ugqhd,ugkhd->ughqk/dot_general | solution.py:27
  45.5 12.1 %divide_reduce_fusion = f32[16,16,8,8]{3,2,1,0:T(8,128)S(1)} fusion(f32[16,16,8,8,8]{3,4,2,1,0:T(8,128)} %fusion.17), kind=kOutput, calls=%fused_computation.18 | output fusion | flops 671758 | bytes 589824 | tf_op jit(solution)/shard_map/div | solution.py:10
  57.8 4.5 %fusion.19 = f32[16,16,8,1,64]{4,3,2,1,0:T(1,128)S(1)} fusion(bf16[16,16,8,8,64]{4,3,2,1,0:T(8,128)(2,1)} %get-tuple-element.138, bf16[16,16,8,8,1]{3,2,1,0,4:T(8,128)(2,1)S(1)} %fusion.26), kind=kOutput, calls=%fused_computation.31 | convolution fusion | flops 2097152 | bytes 2654208 | tf_op jit(solution)/shard_map/ughk,ugkhd->ughd/dot_general | solution.py:32
  71.2 6.3 %copy.93 = bf16[16,16,3,8,2,32]{5,2,1,3,0,4:T(4,128)(2,1)} copy(bf16[16,16,3,8,2,32]{5,4,3,2,1,0:T(2,128)(2,1)} %reshape.219) | data formatting | bytes 1572864 | tf_op jit(solution)/shard_map/reshape | solution.py:94
  77.5 6.6 %reshape.220 = bf16[2,128,16,96]{3,2,1,0:T(8,128)(2,1)S(1)} reshape(bf16[2,16,8,16,3,32]{5,4,3,2,1,0:T(4,128)(2,1)} %bitcast.72) | data formatting | bytes 1572864 | tf_op jit(solution)/shard_map/reshape | solution.py:96
  85.8 16.0 %all_to_all.54 = bf16[2,128,16,96]{1,3,2,0:T(8,128)(2,1)S(1)} all-to-all(bf16[2,128,16,96]{1,3,2,0:T(8,128)(2,1)} %copy.54), channel_id=1, replica_groups=mesh['seq'=128,'head'=2] {'head'}, dimensions={0} | all-to-all | bytes 1572864 | tf_op jit(solution)/shard_map/all_to_all | solution.py:121
  103.5 15.8 %all-to-all-start.1 = ((bf16[1,128,32,96]{3,2,0,1:T(8,128)(2,1)}), bf16[1,128,32,96]{3,2,0,1:T(8,128)(2,1)S(1)}, u32[]{:S(2)}, u32[]{:S(2)}) async-start(bf16[1,128,32,96]{3,2,0,1:T(8,128)(2,1)} %copy.55), calls=%async_computation.1 | async-start | bytes 2097152 | tf_op jit(solution)/shard_map/all_to_all | solution.py:120
  123.1 25.3 %all-to-all-done.1 = bf16[1,128,32,96]{3,2,0,1:T(8,128)(2,1)S(1)} async-done(((bf16[1,128,32,96]{3,2,0,1:T(8,128)(2,1)}), bf16[1,128,32,96]{3,2,0,1:T(8,128)(2,1)S(1)}, u32[]{:S(2)}, u32[]{:S(2)}) %all-to-all-start.1) | async-done | bytes 786464 | tf_op jit(solution)/shard_map/all_to_all | solution.py:120
  152.2 77.0 %all-gather.2.cloned.1.call-done = bf16[16,128,512]{2,0,1:T(8,128)(2,1)} async-done(((bf16[16,1,512]{2,0,1:T(8,128)(2,1)}), bf16[16,128,512]{2,0,1:T(8,128)(2,1)}) %all-gather.2.cloned.1.call-update) | async-done | bytes 2097168 | tf_op jit(solution)/shard_map/all_gather | solution.py:114
  233.1 81.1 %while.22 = (s32[]{:T(128)}, bf16[8,512,32]{1,2,0:T(8,128)(2,1)S(1)}, s32[8]{0:T(128)S(1)}, bf16[4096,32]{1,0:T(8,128)(2,1)}, bf16[4224,32]{1,0:T(8,128)(2,1)S(1...) while((s32[]{:T(128)}, ...), condition=%wide.region_9.10_spmd.clone, body=%wide.region_6.9_spmd.clone.sunk | while | flops 298479488 | bytes 28605896 | solution.py:70
  236.3 3.5 fusion.63
  246.5 3.5 fusion.63
  276.9 3.5 fusion.63
  307.3 3.5 fusion.63
  314.5 3.8 copy.63
  318.9 23.7 %reduce.2 = bf16[4096,32]{1,0:T(8,128)(2,1)S(1)} reduce(bf16[4096,1,1,32]{3,2,1,0:T(2,128)(2,1)} %bitcast.75, bf16[]{:T(256)} %broadcast.255), dimensions={1,2}, to_apply=%bitcast.51.reduce_sub_computation | reduce | bytes 524290
  344.1 9.5 %all-to-all-start.2 = ((bf16[128,2,512]{2,1,0:T(2,128)(2,1)}), bf16[128,2,512]{2,1,0:T(2,128)(2,1)S(1)}, u32[]{:S(2)}, u32[]{:S(2)}) async-start(bf16[128,2,512]{2,1,0:T(2,128)(2,1)} %reshape.324), calls=%async_computation.2 | async-start | bytes 524288 | tf_op jit(solution)/shard_map/all_to_all | solution.py:132
  356.0 11.2 %all-to-all-done.2 = bf16[128,2,512]{2,1,0:T(2,128)(2,1)S(1)} async-done(((bf16[128,2,512]{2,1,0:T(2,128)(2,1)}), bf16[128,2,512]{2,1,0:T(2,128)(2,1)S(1)}, u32[]{:S(2)}, u32[]{:S(2)}) %all-to-all-start.2) | async-done | bytes 262176 | tf_op jit(solution)/shard_map/all_to_all | solution.py:132
  367.2 3.7 reshape.325
  374.3 3.8 all-to-all-start.3
  386.6 3.5 reshape.223
  (130 shorter events, 94.4 us)
Async XLA Ops:
  7.2 1.4 copy-start
  7.2 222.1 %all-gather.2.cloned.1.call-start = ((), (), s32[]{:S(2)}) async-start(), calls=%async_computation.4 | async-start | bytes 2113536 | tf_op jit(solution)/shard_map/all_gather | solution.py:114
  62.3 5.1 %copy-start.3 = (bf16[512,1536]{1,0:T(8,128)(2,1)S(1)}, bf16[512,1536]{1,0:T(8,128)(2,1)}, u32[]{:S(2)}) copy-start(bf16[512,1536]{1,0:T(8,128)(2,1)} %param.18) | copy-start | bytes 4718596
  62.3 5.1 %copy-start.7 = (f32[512]{0:T(512)S(1)}, f32[512]{0:T(512)}, u32[]{:S(2)}) copy-start(f32[512]{0:T(512)} %param.16) | copy-start | bytes 6148
  67.3 10.2 %copy-start.4 = (f32[256,512]{1,0:T(8,128)}, f32[256,512]{1,0:T(8,128)S(1)}, u32[]{:S(2)}) copy-start(f32[256,512]{1,0:T(8,128)S(1)} %get-tuple-element.146) | copy-start | bytes 1572868
  85.8 35.1 %copy-start.9 = (s32[16]{0:T(128)S(1)}, s32[16]{0:T(128)}, u32[]{:S(2)}) copy-start(s32[16]{0:T(128)} %param.13) | copy-start | bytes 196
  103.5 44.9 %all-to-all-start.1 = ((bf16[1,128,32,96]{3,2,0,1:T(8,128)(2,1)}), bf16[1,128,32,96]{3,2,0,1:T(8,128)(2,1)S(1)}, u32[]{:S(2)}, u32[]{:S(2)}) async-start(bf16[1,128,32,96]{3,2,0,1:T(8,128)(2,1)} %copy.55), calls=%async_computation.1 | async-start | bytes 2097152 | tf_op jit(solution)/shard_map/all_to_all | solution.py:120
  148.4 82.5 %copy-start.8 = (f32[512]{0:T(512)S(1)}, f32[512]{0:T(512)}, u32[]{:S(2)}) copy-start(f32[512]{0:T(512)} %param.17) | copy-start | bytes 6148
  239.8 1.3 copy-start.6
  250.0 1.3 copy-start.6
  260.1 1.3 copy-start.6
  270.2 1.3 copy-start.6
  280.4 1.3 copy-start.6
  290.5 1.3 copy-start.6
  300.7 1.3 copy-start.6
  310.8 1.3 copy-start.6
  344.1 23.1 %all-to-all-start.2 = ((bf16[128,2,512]{2,1,0:T(2,128)(2,1)}), bf16[128,2,512]{2,1,0:T(2,128)(2,1)S(1)}, u32[]{:S(2)}, u32[]{:S(2)}) async-start(bf16[128,2,512]{2,1,0:T(2,128)(2,1)} %reshape.324), calls=%async_computation.2 | async-start | bytes 524288 | tf_op jit(solution)/shard_map/all_to_all | solution.py:132
  354.2 1.4 copy-start.2
  374.3 9.4 %all-to-all-start.3 = ((bf16[1,128,32,32]{1,3,0,2:T(8,128)(2,1)}), bf16[1,128,32,32]{1,3,0,2:T(8,128)(2,1)S(1)}, u32[]{:S(2)}, u32[]{:S(2)}) async-start(bf16[1,128,32,32]{1,3,0,2:T(8,128)(2,1)} %copy.65), calls=%async_computation.3 | async-start | bytes 524288 | tf_op jit(solution)/shard_map/all_to_all | solution.py:131
  378.2 14.0 %copy-start.1 = (bf16[512,1536]{1,0:T(8,128)(2,1)S(1)}, bf16[512,1536]{1,0:T(8,128)(2,1)}, u32[]{:S(2)}) copy-start(bf16[512,1536]{1,0:T(8,128)(2,1)} %param.14) | copy-start | bytes 4718596
  380.5 9.7 %copy-start.5 = (f32[256,512]{1,0:T(8,128)S(1)}, f32[256,512]{1,0:T(8,128)}, u32[]{:S(2)}) copy-start(f32[256,512]{1,0:T(8,128)} %copy-done.4) | copy-start | bytes 1572868
Sparse Core Ops, SparseCore 0:
  9.9 219.3 all-gather.1
where the time goes:
time: 405 us; the launch traced here: 399 us
  waiting for transfers between devices  116 us (29%)
  local copies, waits for them, and re-layouts  81 us (20%)
  matrix products  68.8 us (17%)
  other arithmetic  56.7 us (14%)
  starting transfers between devices  29.2 us (7%)
  blocking collectives  16 us (4%)
  loops' own time  16 us (4%)
  between operations  15.3 us (4%)
    all_gather x1, waiting for transfers between devices, per_device(): lax.all_gather(global_tokens, 'seq', axis=1, tiled=True)  77 us
    dot_general x9, matrix products, attend_rows(): jnp.einsum('qd,kd->qk', queries, keys, preferred_element_type=jnp.float32)  28.5 us
    all_to_all x1, waiting for transfers between devices, per_device(): lax.all_to_all(lax.all_to_all(outgoing, 'head', split_axis=0, concat_axis...  25.3 us
    unnamed x1, other arithmetic  23.7 us
    dot_general x9, matrix products, attend_rows(): jnp.dot(weights, values, preferred_element_type=jnp.float32)  18.9 us
    reshape x1, local copies, waits for them, and re-layouts, inner_merge(): flat = flat.reshape(users, groups, 8, 3, 8, head_dim)  16.2 us
    all_to_all x1, blocking collectives, per_device(): lax.all_to_all(outgoing, 'head', split_axis=0, concat_axis=2, tiled=True)  16 us
    another operation x1, loops' own time, pair_attention(): merged_att = lax.map(one_block, starts).reshape(count, head_dim)  16 us
  transfers between devices with their start and end apart: 4, of which 4 were waited for; matrix products, arithmetic and copies ran while one was open for 23% of the time, Pallas kernels for 0%

commit v1 on v0

v1 whole, which is shorter than its diff:
```python
import functools
import math

import jax
import jax.numpy as jnp
from jax import lax
from jax.experimental import pallas as pl
from jax.experimental.pallas import tpu as pltpu
from jax.sharding import PartitionSpec as P

BF16 = jnp.bfloat16
F32 = jnp.float32
USERS = 16
HEADS = 16
WIDTH = 512
HEAD_DIM = 32
GLOBALS = 128
SPAN = 128
TOKENS = 16
DEVICES = 256
COUNT = DEVICES * TOKENS
STEP_USERS = 4
SCORE_SCALE = math.log2(math.e) / math.sqrt(HEAD_DIM)
SAFE = 100.0
LOW = -1e30


def dot_rows(a, b):
    return lax.dot_general(a, b, (((1,), (0,)), ((), ())), preferred_element_type=F32)


def dot_last(a, b):
    return lax.dot_general(a, b, (((1,), (1,)), ((), ())), preferred_element_type=F32)


def iota(shape, axis):
    return lax.broadcasted_iota(jnp.int32, shape, axis)


def norm_f32(wide, gain):
    scale = lax.rsqrt(jnp.mean(wide * wide, axis=-1, keepdims=True) + 1e-06)
    return wide * scale * gain


def inner_kernel(
    events_ref,
    tokens_ref,
    inner_qkv_ref,
    inner_out_ref,
    merge_gain_ref,
    global_gain_ref,
    mixed_qkv_ref,
    merged_ref,
    payload_ref,
    normed_ref,
):
    step = pl.program_id(0)
    x = events_ref[...].reshape(STEP_USERS * SPAN, WIDTH)
    qkv = dot_rows(x, inner_qkv_ref[...]).astype(BF16)
    lane = iota((SPAN, 128), 1)
    low_half = lane < 64
    lane_group8 = iota((8, 128), 1) // 8
    compact = []
    for b in range(STEP_USERS):
        rows = slice(b * SPAN, (b + 1) * SPAN)
        for t in range(4):
            q = qkv[rows, t * 128 : (t + 1) * 128]
            k = qkv[rows, 512 + t * 128 : 512 + (t + 1) * 128]
            zero = jnp.zeros_like(k)
            both = jnp.concatenate(
                [jnp.where(low_half, k, zero), jnp.where(low_half, zero, k)], axis=0
            )
            scores = dot_last(both, q)
            for half in range(2):
                picked = scores[half * 128 : half * 128 + 8]
                for g in range(1, TOKENS):
                    start = half * 128 + g * 8
                    picked = jnp.where(lane_group8 == g, scores[start : start + 8], picked)
                compact.append(picked)
    sc = jnp.stack(compact, axis=0)
    top = jnp.max(sc, axis=1, keepdims=True)
    expd = jnp.exp((sc - top) * 0.125)
    w = expd / jnp.sum(expd, axis=1, keepdims=True)
    w = w.reshape(STEP_USERS * 64, 128)
    same = (iota((128, 128), 0) // 8 == iota((128, 128), 1) // 8).astype(BF16)
    w_hi = w.astype(BF16)
    w_lo = (w - w_hi.astype(F32)).astype(BF16)
    wm = (dot_rows(w_hi, same) + dot_rows(w_lo, same)) * 0.125
    wm = wm.reshape(STEP_USERS * 8, 8, 128)
    on_diag = iota((8, 128), 0) == iota((8, 128), 1) % 8
    row = jnp.sum(jnp.where(on_diag[None], wm, 0.0), axis=1, keepdims=True)
    group_of_lane = iota((TOKENS, 128), 1) // 8 == iota((TOKENS, 128), 0)
    spread = jnp.where(group_of_lane[None], row, 0.0).astype(BF16)
    mean_w = jnp.where(group_of_lane, 0.125, 0.0).astype(BF16)
    low_half16 = iota((TOKENS, 128), 1) < 64
    pooled, means = [], []
    for b in range(STEP_USERS):
        rows = slice(b * SPAN, (b + 1) * SPAN)
        tiles = []
        for t in range(4):
            a = spread[b * 8 + 2 * t : b * 8 + 2 * t + 2].reshape(2 * TOKENS, 128)
            r = dot_rows(a, qkv[rows, 1024 + t * 128 : 1024 + (t + 1) * 128])
            tiles.append(jnp.where(low_half16, r[:TOKENS], r[TOKENS:]))
        pooled.append(jnp.concatenate(tiles, axis=1))
        means.append(dot_rows(mean_w, x[rows]))
    pooled = jnp.concatenate(pooled, axis=0).astype(BF16)
    merged = jnp.concatenate(means, axis=0) + dot_rows(pooled, inner_out_ref[...])
    merged = merged.astype(BF16)
    merged_ref[...] = merged
    rows = STEP_USERS * TOKENS
    normed = norm_f32(merged.astype(F32), merge_gain_ref[...])
    for c in range(4):
        normed_ref[c, pl.ds(pl.multiple_of(step * rows, rows), rows), :] = normed[
            :, c * 128 : (c + 1) * 128
        ]

    @pl.when(step == USERS // STEP_USERS - 1)
    def _():
        slab_rows = jnp.concatenate(
            [
                jnp.concatenate(
                    [normed_ref[c, pl.ds(i, 2 * USERS, stride=8), :] for i in range(8)], axis=0
                ).astype(BF16)
                for c in range(4)
            ],
            axis=1,
        )
        lane_block = iota((2 * USERS, 128), 1) // HEAD_DIM
        for c in range(3):
            for ht in range(4):
                col = c * 512 + ht * 128
                part = dot_rows(slab_rows, mixed_qkv_ref[:, col : col + 128])
                if c == 0:
                    part = part * SCORE_SCALE
                for t in range(2):
                    base = [
                        part[(t * 4 + j) * 2 * USERS : (t * 4 + j + 1) * 2 * USERS]
                        for j in range(4)
                    ]
                    for hh in range(4):
                        out = None
                        for j in range(4):
                            shift = (HEAD_DIM * (j - hh)) % 128
                            moved = pltpu.roll(base[j], shift, 1) if shift else base[j]
                            out = moved if out is None else jnp.where(lane_block == j, moved, out)
                        tile = (c * 2 + t) * 128
                        payload_ref[:, ht * 4 + hh, :, tile : tile + 128] = out.astype(BF16).reshape(
                            USERS, 2, 128
                        )
        gnormed = norm_f32(tokens_ref[...].astype(F32), global_gain_ref[...]).astype(BF16)
        block16 = iota((USERS, 128), 1) // HEAD_DIM
        for ht in range(4):
            sect = []
            for c in range(3):
                col = c * 512 + ht * 128
                part = dot_rows(gnormed, mixed_qkv_ref[:, col : col + 128])
                sect.append(part * SCORE_SCALE if c == 0 else part)
            for hh in range(4):
                out = jnp.zeros((USERS, 128), F32)
                for c in range(3):
                    shift = (HEAD_DIM * (c - hh)) % 128
                    moved = pltpu.roll(sect[c], shift, 1) if shift else sect[c]
                    out = jnp.where(block16 == c, moved, out)
                payload_ref[:, ht * 4 + hh, :, 768:896] = jnp.broadcast_to(
                    out[:, None, :], (USERS, 2, 128)
                ).astype(BF16)


def inner_call(events, tokens, inner_qkv, inner_out, merge_gain, global_gain, mixed_qkv):
    whole = lambda shape: pl.BlockSpec(shape, lambda i: (0,) * len(shape))
    return pl.pallas_call(
        inner_kernel,
        grid=(USERS // STEP_USERS,),
        in_specs=[
            pl.BlockSpec((STEP_USERS, SPAN, WIDTH), lambda i: (i, 0, 0)),
            whole((USERS, WIDTH)),
            whole((WIDTH, 3 * WIDTH)),
            whole((WIDTH, WIDTH)),
            whole((1, WIDTH)),
            whole((1, WIDTH)),
            whole((WIDTH, 3 * WIDTH)),
        ],
        out_specs=[
            pl.BlockSpec((STEP_USERS * TOKENS, WIDTH), lambda i: (i, 0)),
            whole((USERS, HEADS, 2, 896)),
        ],
        out_shape=[
            jax.ShapeDtypeStruct((USERS * TOKENS, WIDTH), BF16),
            jax.ShapeDtypeStruct((USERS, HEADS, 2, 896), BF16),
        ],
        scratch_shapes=[pltpu.VMEM((4, USERS * TOKENS, 128), F32)],
        compiler_params=pltpu.CompilerParams(
            dimension_semantics=("arbitrary",), vmem_limit_bytes=48 * 2**20
        ),
        name="inner",
    )(events, tokens, inner_qkv, inner_out, merge_gain, global_gain, mixed_qkv)


QT = 512
TILES = COUNT // QT
PR = QT // 8


def attend_kernel(valid_ref, recv_ref, att_ref, glob_ref, q_ref, kt_ref, v_ref, g_ref, acc_ref):
    valid = valid_ref[0]
    lane = iota((512, 128), 1)
    first = lane < HEAD_DIM
    ones = jnp.where(lane == HEAD_DIM, 1.0, 0.0)
    prow = iota((512, 128), 0)
    same = (iota((128, 128), 0) // HEAD_DIM == iota((128, 128), 1) // HEAD_DIM).astype(BF16)

    def tile_of(index):
        return recv_ref[:, :, index * 128 : (index + 1) * 128].reshape(512, 128)

    def top_square(x):
        return jnp.max(dot_rows((x * x).astype(BF16), same))

    g_ref[...] = tile_of(6).astype(F32)
    g = g_ref[pl.ds(0, GLOBALS, stride=4), :]
    g_lane = iota((GLOBALS, 128), 1)
    gq = g.astype(BF16)[:, :HEAD_DIM]
    gkt = g.T.astype(BF16)[HEAD_DIM : 2 * HEAD_DIM]
    gv = jnp.where(g_lane < HEAD_DIM, pltpu.roll(g, 64, 1), jnp.where(g_lane == HEAD_DIM, 1.0, 0.0))
    gv = gv.astype(BF16)
    g_sq = dot_rows((g * g).astype(BF16), same)
    q_top = jnp.max(jnp.where(g_lane < HEAD_DIM, g_sq, 0.0))
    k_top = jnp.max(jnp.where(g_lane // HEAD_DIM == 1, g_sq, 0.0))

    for t in range(2):
        q = tile_of(t).astype(F32)
        k = tile_of(2 + t).astype(F32)
        v = tile_of(4 + t).astype(F32)
        q_top = jnp.maximum(q_top, top_square(q))
        k_top = jnp.maximum(k_top, top_square(k))
        k_t = k.T.astype(BF16)
        for j in range(4):
            i = t * 4 + j
            qi = (pltpu.roll(q, 128 - 32 * j, 1) if j else q).astype(BF16)
            vi = pltpu.roll(v, 128 - 32 * j, 1) if j else v
            vi = jnp.where(prow * 8 + i < valid, jnp.where(first, vi, ones), 0.0).astype(BF16)
            ki = k_t[j * HEAD_DIM : (j + 1) * HEAD_DIM]
            for n in range(TILES):
                at = n * QT + i * PR
                q_ref[at : at + PR, :] = qi[n * PR : (n + 1) * PR]
                v_ref[at : at + PR, :] = vi[n * PR : (n + 1) * PR]
                kt_ref[n, :, i * PR : (i + 1) * PR] = ki[:, n * PR : (n + 1) * PR]

    def place(index):
        return (index % PR) * 8 + index // PR

    out_lane = iota((PR, 128), 1) // HEAD_DIM

    def finish(n, acc):
        o = acc / acc[:, HEAD_DIM : HEAD_DIM + 1]
        for t in range(2):
            packed = o[t * 4 * PR : (t * 4 + 1) * PR]
            for j in range(1, 4):
                i = t * 4 + j
                packed = jnp.where(
                    out_lane == j, pltpu.roll(o[i * PR : (i + 1) * PR], 32 * j, 1), packed
                )
            att_ref[pl.ds(n * (PR // 2), PR // 2), :, t * 128 : (t + 1) * 128] = packed.astype(
                BF16
            ).reshape(PR // 2, 2, 128)

    safe = q_top * k_top * 1.05 < SAFE * SAFE

    @pl.when(safe)
    def _():
        causal = place(iota((QT, QT), 0)) >= place(iota((QT, QT), 1))
        for n in range(TILES):
            q = q_ref[n * QT : (n + 1) * QT, :HEAD_DIM]
            p = jnp.exp2(dot_rows(q, gkt)).astype(BF16)
            acc_ref[...] = dot_rows(p, gv)

            def body(m, carry, q=q):
                s = dot_rows(q, kt_ref[m])
                p = jnp.exp2(s).astype(BF16)
                at = pl.multiple_of(m * QT, QT)
                acc_ref[...] += dot_rows(p, v_ref[pl.ds(at, QT), :])
                return carry

            lax.fori_loop(0, n, body, 0)
            s = dot_rows(q, kt_ref[n])
            p = jnp.where(causal, jnp.exp2(s), 0.0).astype(BF16)
            finish(n, acc_ref[...] + dot_rows(p, v_ref[n * QT : (n + 1) * QT, :]))
        p = jnp.exp2(dot_rows(gq, gkt)).astype(BF16)

        def gbody(m, acc):
            p = jnp.exp2(dot_rows(gq, kt_ref[m])).astype(BF16)
            at = pl.multiple_of(m * QT, QT)
            return acc + dot_rows(p, v_ref[pl.ds(at, QT), :])

        acc = lax.fori_loop(0, TILES, gbody, dot_rows(p, gv))
        o = acc / acc[:, HEAD_DIM : HEAD_DIM + 1]
        glob_ref[...] = o[:, :HEAD_DIM].astype(BF16)

    @pl.when(jnp.logical_not(safe))
    def _():
        def shifted(s, allowed, vals, state):
            top, acc = state
            if allowed is not None:
                s = jnp.where(allowed, s, LOW)
            new = jnp.maximum(top, jnp.max(s, axis=1, keepdims=True))
            p = jnp.exp2(s - new).astype(BF16)
            return new, acc * jnp.exp2(top - new) + dot_rows(p, vals)

        def start(q):
            rows = q.shape[0]
            state = (jnp.full((rows, 1), LOW, F32), jnp.zeros((rows, 128), F32))
            return shifted(dot_rows(q, gkt), None, gv, state)

        def tile(n, carry):
            q = q_ref[pl.ds(pl.multiple_of(n * QT, QT), QT), :][:, :HEAD_DIM]

            def body(m, state):
                row = n * QT + place(iota((QT, QT), 0))
                column = m * QT + place(iota((QT, QT), 1))
                allowed = (row >= column) & (column < valid)
                vals = v_ref[pl.ds(pl.multiple_of(m * QT, QT), QT), :]
                return shifted(dot_rows(q, kt_ref[m]), allowed, vals, state)

            finish(n, lax.fori_loop(0, n + 1, body, start(q))[1])
            return carry

        lax.fori_loop(0, TILES, tile, 0)

        def gbody(m, state):
            allowed = m * QT + place(iota((GLOBALS, QT), 1)) < valid
            vals = v_ref[pl.ds(pl.multiple_of(m * QT, QT), QT), :]
            return shifted(dot_rows(gq, kt_ref[m]), allowed, vals, state)

        acc = lax.fori_loop(0, TILES, gbody, start(gq))[1]
        o = acc / acc[:, HEAD_DIM : HEAD_DIM + 1]
        glob_ref[...] = o[:, :HEAD_DIM].astype(BF16)


def attend_call(valid, recv):
    vmem = pl.BlockSpec(memory_space=pltpu.VMEM)
    return pl.pallas_call(
        attend_kernel,
        in_specs=[pl.BlockSpec(memory_space=pltpu.SMEM), vmem],
        out_specs=[vmem, vmem],
        out_shape=[
            jax.ShapeDtypeStruct((DEVICES, 2, 256), BF16),
            jax.ShapeDtypeStruct((GLOBALS, HEAD_DIM), BF16),
        ],
        scratch_shapes=[
            pltpu.VMEM((COUNT, 128), BF16),
            pltpu.VMEM((TILES, HEAD_DIM, QT), BF16),
            pltpu.VMEM((COUNT, 128), BF16),
            pltpu.VMEM((512, 128), F32),
            pltpu.VMEM((QT, 128), F32),
        ],
        compiler_params=pltpu.CompilerParams(vmem_limit_bytes=48 * 2**20),
        name="attend",
    )(valid, recv)


def output_kernel(back_ref, merged_ref, mixed_out_ref, out_ref, wide_ref, sum_ref):
    for h in range(HEADS):
        rows = mixed_out_ref[h * HEAD_DIM : (h + 1) * HEAD_DIM, :]
        for j in range(4):
            wide_ref[h * 128 + j * HEAD_DIM : h * 128 + (j + 1) * HEAD_DIM, :] = rows
    block = iota((2 * USERS, 128), 1) // HEAD_DIM
    keep = [(block == j).astype(F32).astype(BF16) for j in range(4)]
    parts = [[] for _ in range(8)]
    for h in range(HEADS):
        for t in range(2):
            x = back_ref[:, h, :, t * 128 : (t + 1) * 128].reshape(2 * USERS, 128)
            for j in range(4):
                parts[t * 4 + j].append(x * keep[j])
    lhs = jnp.concatenate([jnp.concatenate(p, axis=1) for p in parts], axis=0)
    prod = dot_rows(lhs, wide_ref[...])
    for c in range(4):
        cols = slice(c * 128, (c + 1) * 128)
        for i in range(8):
            rows = slice(i * 2 * USERS, (i + 1) * 2 * USERS)
            sum_ref[c, pl.ds(i, 2 * USERS, stride=8), :] = prod[rows, cols]
        out_ref[:, cols] = (merged_ref[:, cols].astype(F32) + sum_ref[c]).astype(BF16)


def output_call(back, merged, mixed_out):
    vmem = pl.BlockSpec(memory_space=pltpu.VMEM)
    return pl.pallas_call(
        output_kernel,
        in_specs=[vmem] * 3,
        out_specs=vmem,
        out_shape=jax.ShapeDtypeStruct((USERS * TOKENS, WIDTH), BF16),
        scratch_shapes=[
            pltpu.VMEM((HEADS * 128, WIDTH), BF16),
            pltpu.VMEM((4, USERS * TOKENS, 128), F32),
        ],
        compiler_params=pltpu.CompilerParams(vmem_limit_bytes=48 * 2**20),
        name="output",
    )(back, merged, mixed_out)


def per_device(
    events,
    global_tokens,
    lengths,
    inner_qkv,
    inner_out,
    merge_gain,
    global_gain,
    mixed_qkv,
    mixed_out,
):
    merged, payload = inner_call(
        events,
        global_tokens.reshape(USERS, WIDTH),
        inner_qkv,
        inner_out,
        merge_gain.reshape(1, WIDTH),
        global_gain.reshape(1, WIDTH),
        mixed_qkv,
    )
    arrived = lax.all_to_all(
        payload.reshape(DEVICES, 2, 896), ("seq", "head"), split_axis=0, concat_axis=0, tiled=True
    )
    user = lax.axis_index("seq") // 8
    valid = lax.dynamic_slice_in_dim(lengths, user, 1) // 8
    att, glob = attend_call(valid, arrived)
    back = lax.all_to_all(att, ("seq", "head"), split_axis=0, concat_axis=0, tiled=True)
    out = output_call(back.reshape(USERS, HEADS, 2, 256), merged, mixed_out)
    return (out.reshape(USERS, TOKENS, WIDTH), glob.reshape(1, 1, GLOBALS * HEAD_DIM))


def solution(mesh):
    in_specs = (
        P(None, ("seq", "head"), None),
        P(None, "seq", None),
        P(),
        P(),
        P(),
        P(),
        P(),
        P(),
        P(),
    )
    out_specs = (P(None, ("seq", "head"), None), P("seq", "head", None))
    return jax.shard_map(
        per_device, mesh=mesh, in_specs=in_specs, out_specs=out_specs, check_vma=False
    )
```

time: 405 us -> 119 us (0.29); the launches traced: 399 us -> 119 us
  waiting for transfers between devices: 116 us -> 39.8 us
  local copies, waits for them, and re-layouts: 81 us -> 7.22 us
  matrix products: 68.8 us -> 0 us
  other arithmetic: 56.7 us -> 0 us
  Pallas kernels: 0 us -> 46.6 us
  loops' own time: 16 us -> 0 us
  blocking collectives: 16 us -> 0 us
  between operations: 15.3 us -> 3.3 us
  starting transfers between devices: 29.2 us -> 21.9 us
    all_gather x1 -> x0, waiting for transfers between devices: 77 us -> none  [per_device(): lax.all_gather(global_tokens, 'seq', axis=1, tiled=True)]
    dot_general x25 -> x0, matrix products: 68.8 us -> none  [the longest x9 28.5 us: attend_rows(): jnp.einsum('qd,kd->qk', queries, keys, preferred_element_type=jnp.float32)]
    pallas_call x0 -> x3, Pallas kernels: none -> 46.6 us  [the longest x1 33.5 us: attend_call(): pl.pallas_call(attend_kernel, in_specs=[pl.BlockSpec(memory_space=pltpu.S...]
    reshape x8 -> x1, local copies, waits for them, and re-layouts: 38.7 us -> 0.7 us  [per_device(): glob.reshape(1, 1, GLOBALS * HEAD_DIM)]
    unnamed x1 -> x0, other arithmetic: 23.7 us -> none
    all_to_all x1 -> x0, blocking collectives: 16 us -> none  [per_device(): lax.all_to_all(outgoing, 'head', split_axis=0, concat_axis=2, tiled=True)]
    another operation x1 -> x0, loops' own time: 16 us -> none  [pair_attention(): merged_att = lax.map(one_block, starts).reshape(count, head_dim)]
    reduce_sum x11 -> x0, other arithmetic: 14.4 us -> none  [the longest x9 11.1 us: softmax_last(): return expd / jnp.sum(expd, axis=-1, keepdims=True)]
  transfers between devices with their start and end apart: 4 -> 2, of which waited for: 4 -> 2; matrix products, arithmetic and copies ran while one was open for 23% -> 1% of each run, Pallas kernels for 0% -> 0%
where the time goes in v1:
time: 119 us
  Pallas kernels  46.6 us (39%)
  waiting for transfers between devices  39.8 us (33%)
  starting transfers between devices  21.9 us (18%)
  local copies, waits for them, and re-layouts  7.22 us (6%)
  between operations  3.3 us (3%)
    pallas_call x1, Pallas kernels, attend_call(): pl.pallas_call(attend_kernel, in_specs=[pl.BlockSpec(memory_space=pltpu.S...  33.5 us
    all_to_all x1, waiting for transfers between devices, per_device(): lax.all_to_all(payload.reshape(DEVICES, 2, 896), ('seq', 'head'), split_a...  25.4 us
    all_to_all x1, starting transfers between devices, per_device(): lax.all_to_all(payload.reshape(DEVICES, 2, 896), ('seq', 'head'), split_a...  15.7 us
    all_to_all x1, waiting for transfers between devices, per_device(): lax.all_to_all(att, ('seq', 'head'), split_axis=0, concat_axis=0, tiled=T...  14.4 us
    pallas_call x1, Pallas kernels, inner_call(): pl.pallas_call(inner_kernel, grid=(USERS // STEP_USERS,), in_specs=[pl.Bl...  11.4 us
    all_to_all x1, starting transfers between devices, per_device(): lax.all_to_all(att, ('seq', 'head'), split_axis=0, concat_axis=0, tiled=T...  6.23 us
    unnamed x16, local copies, waits for them, and re-layouts  5.94 us
  transfers between devices with their start and end apart: 2, of which 2 were waited for; matrix products, arithmetic and copies ran while one was open for 1% of the time, Pallas kernels for 0%

profile of v1, /device:TPU:1, one launch (start us, length us, event | category | flops | bytes accessed | tf_op | source)
XLA Modules:
  0.0 118.8 jit_solution(6872536677712222009)
XLA Ops:
  0.6 0.0 copy-start
  0.6 1.4 %copy-done = bf16[512,1536]{1,0:T(8,128)(2,1)S(1)} copy-done((bf16[512,1536]{1,0:T(8,128)(2,1)S(1)}, bf16[512,1536]{1,0:T(8,128)(2,1)}, u32[]{:S(2)}) %copy-start) | copy-done | bytes 1572888
  2.0 0.0 copy-start.1
  2.0 1.4 %copy-done.1 = bf16[512,1536]{1,0:T(8,128)(2,1)S(1)} copy-done((bf16[512,1536]{1,0:T(8,128)(2,1)S(1)}, bf16[512,1536]{1,0:T(8,128)(2,1)}, u32[]{:S(2)}) %copy-start.1) | copy-done | bytes 1572888
  3.4 0.0 copy-start.2
  3.5 1.0 copy-done.2
  4.5 0.0 copy-start.4
  4.5 0.7 copy-done.4
  5.2 0.0 copy-start.5
  5.2 0.7 copy-done.5
  5.9 0.0 copy-start.6
  5.9 0.7 copy-done.6
  6.6 11.4 %inner.1 = (bf16[256,512]{1,0:T(8,128)(2,1)S(1)}, bf16[16,16,2,896]{3,2,1,0:T(2,128)(2,1)}) custom-call(bf16[16,128,512]{2,1,0:T(8,128)(2,1)} %events_ref.1, bf16[16,512]{1,0:T(8,128)(2,1)S(1)} %bitcast.7, bf16[512,1536]{1,0:T(8,128)(2,1)S(1)} %copy-done, bf16[512,512]{1,0:T(8,128)(2,1)S(1)} %copy-done.2, f32[1,512]{1,0:T(1,128)S(1)} %bitcast.8, ...), custom_call_target="tpu_custom_call" | custom-call | tf_op jit(solution)/shard_map/inner/pallas_call | solution.py:171
  18.0 0.0 copy-start.7
  18.0 15.7 %all-to-all-start = ((bf16[256,2,896]{2,1,0:T(2,128)(2,1)}), bf16[256,2,896]{2,1,0:T(2,128)(2,1)S(1)}, u32[]{:S(2)}, u32[]{:S(2)}) async-start(bf16[256,2,896]{2,1,0:T(2,128)(2,1)} %bitcast.3), calls=%async_computation | async-start | bytes 1835008 | tf_op jit(solution)/shard_map/all_to_all | solution.py:419
  33.7 0.0 copy-done.7
  33.7 0.6 dynamic_slice.3
  36.9 25.4 %all-to-all-done.recv_ref = bf16[256,2,896]{2,1,0:T(2,128)(2,1)S(1)} async-done(((bf16[256,2,896]{2,1,0:T(2,128)(2,1)}), bf16[256,2,896]{2,1,0:T(2,128)(2,1)S(1)}, u32[]{:S(2)}, u32[]{:S(2)}) %all-to-all-start) | async-done | bytes 917536 | tf_op jit(solution)/shard_map/all_to_all | solution.py:419
  62.3 33.5 %attend.1 = (bf16[256,2,256]{2,1,0:T(2,128)(2,1)}, bf16[128,32]{1,0:T(8,128)(2,1)S(1)}) custom-call(s32[1]{0:T(128)S(6)} %select_n.15.valid_ref, bf16[256,2,896]{2,1,0:T(2,128)(2,1)S(1)} %all-to-all-done.recv_ref), custom_call_target="tpu_custom_call" | custom-call | tf_op jit(solution)/shard_map/attend/pallas_call | solution.py:340
  95.7 6.2 %all-to-all-start.1 = ((bf16[256,2,256]{2,1,0:T(2,128)(2,1)}), bf16[256,2,256]{2,1,0:T(2,128)(2,1)S(1)}, u32[]{:S(2)}, u32[]{:S(2)}) async-start(bf16[256,2,256]{2,1,0:T(2,128)(2,1)} %get-tuple-element.7), calls=%async_computation.1 | async-start | bytes 524288 | tf_op jit(solution)/shard_map/all_to_all | solution.py:425
  102.0 0.7 reshape.35
  102.7 14.4 %all-to-all-done.1 = bf16[256,2,256]{2,1,0:T(2,128)(2,1)S(1)} async-done(((bf16[256,2,256]{2,1,0:T(2,128)(2,1)}), bf16[256,2,256]{2,1,0:T(2,128)(2,1)S(1)}, u32[]{:S(2)}, u32[]{:S(2)}) %all-to-all-start.1) | async-done | bytes 262176 | tf_op jit(solution)/shard_map/all_to_all | solution.py:425
  117.1 0.0 copy-done.3
  117.1 1.7 %output.1 = bf16[256,512]{1,0:T(8,128)(2,1)} custom-call(bf16[16,16,2,256]{3,2,1,0:T(2,128)(2,1)S(1)} %bitcast.6, bf16[256,512]{1,0:T(8,128)(2,1)S(1)} %get-tuple-element.8.merged_ref, bf16[512,512]{1,0:T(8,128)(2,1)S(1)} %copy-done.3), custom_call_target="tpu_custom_call" | custom-call | tf_op jit(solution)/shard_map/output/pallas_call | solution.py:385
  (1 shorter events, 0.0 us)
Async XLA Ops:
  0.6 1.4 %copy-start = (bf16[512,1536]{1,0:T(8,128)(2,1)S(1)}, bf16[512,1536]{1,0:T(8,128)(2,1)}, u32[]{:S(2)}) copy-start(bf16[512,1536]{1,0:T(8,128)(2,1)} %inner_qkv_ref.1) | copy-start | bytes 4718596
  2.0 1.4 %copy-start.1 = (bf16[512,1536]{1,0:T(8,128)(2,1)S(1)}, bf16[512,1536]{1,0:T(8,128)(2,1)}, u32[]{:S(2)}) copy-start(bf16[512,1536]{1,0:T(8,128)(2,1)} %mixed_qkv_ref.1) | copy-start | bytes 4718596
  3.4 1.0 copy-start.2
  4.5 0.7 copy-start.4
  5.2 0.7 copy-start.5
  5.9 0.7 copy-start.6
  18.0 15.7 %copy-start.7 = (s32[16]{0:T(128)S(1)}, s32[16]{0:T(128)}, u32[]{:S(2)}) copy-start(s32[16]{0:T(128)} %param.11) | copy-start | bytes 196
  18.0 99.1 %copy-start.3 = (bf16[512,512]{1,0:T(8,128)(2,1)S(1)}, bf16[512,512]{1,0:T(8,128)(2,1)}, u32[]{:S(2)}) copy-start(bf16[512,512]{1,0:T(8,128)(2,1)} %mixed_out_ref.1) | copy-start | bytes 1572868
  18.0 44.3 %all-to-all-start = ((bf16[256,2,896]{2,1,0:T(2,128)(2,1)}), bf16[256,2,896]{2,1,0:T(2,128)(2,1)S(1)}, u32[]{:S(2)}, u32[]{:S(2)}) async-start(bf16[256,2,896]{2,1,0:T(2,128)(2,1)} %bitcast.3), calls=%async_computation | async-start | bytes 1835008 | tf_op jit(solution)/shard_map/all_to_all | solution.py:419
  95.7 21.4 %all-to-all-start.1 = ((bf16[256,2,256]{2,1,0:T(2,128)(2,1)}), bf16[256,2,256]{2,1,0:T(2,128)(2,1)S(1)}, u32[]{:S(2)}, u32[]{:S(2)}) async-start(bf16[256,2,256]{2,1,0:T(2,128)(2,1)} %get-tuple-element.7), calls=%async_computation.1 | async-start | bytes 524288 | tf_op jit(solution)/shard_map/all_to_all | solution.py:425

commit v2 on v1

v2 whole, which is shorter than its diff:
```python
import functools
import math

import jax
import jax.numpy as jnp
from jax import lax
from jax.experimental import pallas as pl
from jax.experimental.pallas import tpu as pltpu
from jax.sharding import PartitionSpec as P

BF16 = jnp.bfloat16
F32 = jnp.float32
USERS = 16
HEADS = 16
WIDTH = 512
HEAD_DIM = 32
GLOBALS = 128
SPAN = 128
TOKENS = 16
DEVICES = 256
COUNT = DEVICES * TOKENS
STEP_USERS = 4
SCORE_SCALE = math.log2(math.e) / math.sqrt(HEAD_DIM)
SAFE = 100.0
LOW = -1e30


def dot_rows(a, b):
    return lax.dot_general(a, b, (((1,), (0,)), ((), ())), preferred_element_type=F32)


def dot_last(a, b):
    return lax.dot_general(a, b, (((1,), (1,)), ((), ())), preferred_element_type=F32)


def iota(shape, axis):
    return lax.broadcasted_iota(jnp.int32, shape, axis)


def norm_f32(wide, gain):
    scale = lax.rsqrt(jnp.mean(wide * wide, axis=-1, keepdims=True) + 1e-06)
    return wide * scale * gain


def inner_kernel(
    events_ref,
    tokens_hbm,
    inner_qkv_hbm,
    inner_out_hbm,
    merge_gain_hbm,
    global_gain_hbm,
    mixed_qkv_hbm,
    merged_ref,
    payload_ref,
    normed_ref,
    tokens_ref,
    inner_qkv_ref,
    inner_out_ref,
    merge_gain_ref,
    global_gain_ref,
    mixed_qkv_ref,
    sems,
):
    step = pl.program_id(0)
    fetch = []
    for c in range(3):
        cols = slice(c * WIDTH, (c + 1) * WIDTH)
        fetch.append((inner_qkv_hbm.at[:, cols], inner_qkv_ref.at[:, cols]))
    fetch.append((inner_out_hbm, inner_out_ref))
    fetch.append((merge_gain_hbm, merge_gain_ref))
    for c in range(3):
        cols = slice(c * WIDTH, (c + 1) * WIDTH)
        fetch.append((mixed_qkv_hbm.at[:, cols], mixed_qkv_ref.at[:, cols]))
    fetch.append((tokens_hbm, tokens_ref))
    fetch.append((global_gain_hbm, global_gain_ref))
    copies = [
        pltpu.make_async_copy(src, dst, sems.at[n]) for n, (src, dst) in enumerate(fetch)
    ]

    @pl.when(step == 0)
    def _():
        for copy in copies:
            copy.start()
        for copy in copies[:3]:
            copy.wait()

    x = events_ref[...].reshape(STEP_USERS * SPAN, WIDTH)
    qkv = dot_rows(x, inner_qkv_ref[...]).astype(BF16)
    lane = iota((SPAN, 128), 1)
    low = (lane < 64).astype(F32).astype(BF16)
    high = (lane >= 64).astype(F32).astype(BF16)
    lane_group8 = iota((8, 128), 1) // 8
    compact = []
    for b in range(STEP_USERS):
        rows = slice(b * SPAN, (b + 1) * SPAN)
        for t in range(4):
            q = qkv[rows, t * 128 : (t + 1) * 128]
            k = qkv[rows, 512 + t * 128 : 512 + (t + 1) * 128]
            scores = dot_last(k, jnp.concatenate([q * low, q * high], axis=0))
            for half in range(2):
                part = scores[:, half * 128 : (half + 1) * 128]
                picked = part[0:8]
                for g in range(1, TOKENS):
                    picked = jnp.where(lane_group8 == g, part[g * 8 : g * 8 + 8], picked)
                compact.append(picked)
    sc = jnp.stack(compact, axis=0)
    top = jnp.max(sc, axis=1, keepdims=True)
    expd = jnp.exp((sc - top) * 0.125)
    w = expd / jnp.sum(expd, axis=1, keepdims=True)
    w = w.reshape(STEP_USERS * 64, 128)
    same = (iota((128, 128), 0) // 8 == iota((128, 128), 1) // 8).astype(BF16)
    w_hi = w.astype(BF16)
    w_lo = (w - w_hi.astype(F32)).astype(BF16)
    wm = (dot_rows(w_hi, same) + dot_rows(w_lo, same)) * 0.125
    wm = wm.reshape(STEP_USERS * 8, 8, 128)
    on_diag = iota((8, 128), 0) == iota((8, 128), 1) % 8
    row = jnp.sum(jnp.where(on_diag[None], wm, 0.0), axis=1, keepdims=True)
    group_of_lane = iota((TOKENS, 128), 1) // 8 == iota((TOKENS, 128), 0)
    spread = jnp.where(group_of_lane[None], row, 0.0).astype(BF16)
    mean_w = jnp.where(group_of_lane, 0.125, 0.0).astype(BF16)
    low_half = iota((TOKENS, 128), 1) < 64
    pooled, means = [], []
    for b in range(STEP_USERS):
        rows = slice(b * SPAN, (b + 1) * SPAN)
        tiles = []
        for tp in range(2):
            a = spread[b * 8 + 4 * tp : b * 8 + 4 * tp + 4].reshape(4 * TOKENS, 128)
            r = dot_rows(a, qkv[rows, 1024 + tp * 256 : 1024 + (tp + 1) * 256])
            for t in range(2):
                cols = slice(t * 128, (t + 1) * 128)
                at = 2 * t * TOKENS
                tiles.append(
                    jnp.where(low_half, r[at : at + TOKENS, cols], r[at + TOKENS : at + 2 * TOKENS, cols])
                )
        pooled.append(jnp.concatenate(tiles, axis=1))
        means.append(dot_rows(mean_w, x[rows]))
    pooled = jnp.concatenate(pooled, axis=0).astype(BF16)

    @pl.when(step == 0)
    def _():
        for copy in copies[3:5]:
            copy.wait()

    merged = jnp.concatenate(means, axis=0) + dot_rows(pooled, inner_out_ref[...])
    merged = merged.astype(BF16)
    merged_ref[...] = merged
    rows = STEP_USERS * TOKENS
    normed = norm_f32(merged.astype(F32), merge_gain_ref[...])
    for c in range(4):
        normed_ref[c, pl.ds(pl.multiple_of(step * rows, rows), rows), :] = normed[
            :, c * 128 : (c + 1) * 128
        ]

    @pl.when(step == USERS // STEP_USERS - 1)
    def _():
        for copy in copies[5:]:
            copy.wait()
        slab_rows = jnp.concatenate(
            [
                jnp.concatenate(
                    [normed_ref[c, pl.ds(i, 2 * USERS, stride=8), :] for i in range(8)], axis=0
                ).astype(BF16)
                for c in range(4)
            ],
            axis=1,
        )
        lane_block = iota((2 * USERS, 128), 1) // HEAD_DIM
        for c in range(3):
            for hp in range(2):
                col = c * 512 + hp * 256
                pair = dot_rows(slab_rows, mixed_qkv_ref[:, col : col + 256])
                if c == 0:
                    pair = pair * SCORE_SCALE
                for ht in (2 * hp, 2 * hp + 1):
                    part = pair[:, (ht % 2) * 128 : (ht % 2 + 1) * 128]
                    for t in range(2):
                        base = [
                            part[(t * 4 + j) * 2 * USERS : (t * 4 + j + 1) * 2 * USERS]
                            for j in range(4)
                        ]
                        for hh in range(4):
                            out = None
                            for j in range(4):
                                shift = (HEAD_DIM * (j - hh)) % 128
                                moved = pltpu.roll(base[j], shift, 1) if shift else base[j]
                                out = moved if j == 0 else jnp.where(lane_block == j, moved, out)
                            tile = (c * 2 + t) * 128
                            payload_ref[:, ht * 4 + hh, :, tile : tile + 128] = out.astype(
                                BF16
                            ).reshape(USERS, 2, 128)
        gnormed = norm_f32(tokens_ref[...].astype(F32), global_gain_ref[...]).astype(BF16)
        block16 = iota((USERS, 128), 1) // HEAD_DIM
        gqkv = [
            dot_rows(gnormed, mixed_qkv_ref[:, c * 512 : (c + 1) * 512]) for c in range(3)
        ]
        gqkv[0] = gqkv[0] * SCORE_SCALE
        for ht in range(4):
            sect = [part[:, ht * 128 : (ht + 1) * 128] for part in gqkv]
            for hh in range(4):
                out = jnp.zeros((USERS, 128), F32)
                for c in range(3):
                    shift = (HEAD_DIM * (c - hh)) % 128
                    moved = pltpu.roll(sect[c], shift, 1) if shift else sect[c]
                    out = jnp.where(block16 == c, moved, out)
                payload_ref[:, ht * 4 + hh, :, 768:896] = jnp.broadcast_to(
                    out[:, None, :], (USERS, 2, 128)
                ).astype(BF16)


def inner_call(events, tokens, inner_qkv, inner_out, merge_gain, global_gain, mixed_qkv):
    hbm = pl.BlockSpec(memory_space=pl.ANY)
    return pl.pallas_call(
        inner_kernel,
        grid=(USERS // STEP_USERS,),
        in_specs=[pl.BlockSpec((STEP_USERS, SPAN, WIDTH), lambda i: (i, 0, 0))] + [hbm] * 6,
        out_specs=[
            pl.BlockSpec((STEP_USERS * TOKENS, WIDTH), lambda i: (i, 0)),
            pl.BlockSpec((USERS, HEADS, 2, 896), lambda i: (0, 0, 0, 0)),
        ],
        out_shape=[
            jax.ShapeDtypeStruct((USERS * TOKENS, WIDTH), BF16),
            jax.ShapeDtypeStruct((USERS, HEADS, 2, 896), BF16),
        ],
        scratch_shapes=[
            pltpu.VMEM((4, USERS * TOKENS, 128), F32),
            pltpu.VMEM((USERS, WIDTH), BF16),
            pltpu.VMEM((WIDTH, 3 * WIDTH), BF16),
            pltpu.VMEM((WIDTH, WIDTH), BF16),
            pltpu.VMEM((1, WIDTH), F32),
            pltpu.VMEM((1, WIDTH), F32),
            pltpu.VMEM((WIDTH, 3 * WIDTH), BF16),
            pltpu.SemaphoreType.DMA((10,)),
        ],
        compiler_params=pltpu.CompilerParams(
            dimension_semantics=("arbitrary",), vmem_limit_bytes=60 * 2**20
        ),
        name="inner",
    )(events, tokens, inner_qkv, inner_out, merge_gain, global_gain, mixed_qkv)


QT = 512
TILES = COUNT // QT
PR = QT // 8
VROWS = 48
QUERIES = COUNT + GLOBALS


def place(index):
    return (index % PR) * 8 + index // PR


def attend_kernel(lengths_ref, recv_ref, att_ref, glob_ref, qt_ref, k_ref, vt_ref, g_ref, acc_ref):
    valid = lengths_ref[lax.axis_index("seq") // 8] // 8
    prow = iota((HEAD_DIM, 512), 1)
    same = (iota((128, 128), 0) // HEAD_DIM == iota((128, 128), 1) // HEAD_DIM).astype(BF16)

    def tile_of(index):
        return recv_ref[:, :, index * 128 : (index + 1) * 128].reshape(512, 128)

    g_ref[...] = tile_of(6).astype(F32)
    g = g_ref[pl.ds(0, GLOBALS, stride=4), :]
    gt = g.T
    gk = pltpu.roll(g, 128 - HEAD_DIM, 1).astype(BF16)[:, :HEAD_DIM]
    qt_ref[:, COUNT:] = gt[:HEAD_DIM].astype(BF16)
    one_row = jnp.where(iota((VROWS - HEAD_DIM, GLOBALS), 0) == 0, 1.0, 0.0)
    gvt = jnp.concatenate([gt[2 * HEAD_DIM : 3 * HEAD_DIM], one_row], axis=0).astype(BF16)
    tail_row = iota((VROWS - HEAD_DIM, 512), 0) == 0
    gg = g * g
    g_sq = dot_rows(gg.astype(BF16), same)
    g_lane = iota((GLOBALS, 128), 1) // HEAD_DIM
    k_top = jnp.max(jnp.where(g_lane == 1, g_sq, 0.0))

    for t in range(2):
        q_t = tile_of(t).astype(F32).T.astype(BF16)
        v_t = tile_of(4 + t).astype(F32).T
        k = tile_of(2 + t).astype(F32)
        k_top = jnp.maximum(k_top, jnp.max(dot_rows((k * k).astype(BF16), same)))
        for j in range(4):
            i = t * 4 + j
            band = slice(j * HEAD_DIM, (j + 1) * HEAD_DIM)
            live = prow * 8 + i < valid
            vi = jnp.where(live, v_t[band], 0.0)
            tail = jnp.where(tail_row & live[: VROWS - HEAD_DIM], 1.0, 0.0)
            vi = jnp.concatenate([vi, tail], axis=0).astype(BF16)
            ki = (pltpu.roll(k, 128 - j * HEAD_DIM, 1) if j else k).astype(BF16)
            for n in range(TILES):
                at = n * QT + i * PR
                part = slice(n * PR, (n + 1) * PR)
                qt_ref[:, at : at + PR] = q_t[band, part]
                vt_ref[n, :, i * PR : (i + 1) * PR] = vi[:, part]
                k_ref[at : at + PR, :] = ki[part]

    q_all = qt_ref[...].astype(F32)
    q_top = jnp.max(jnp.sum(q_all * q_all, axis=0, keepdims=True))
    safe = q_top * k_top * 1.05 < SAFE * SAFE

    @pl.when(safe)
    def _():
        acc_ref[...] = dot_rows(gvt, jnp.exp2(dot_rows(gk, qt_ref[...])).astype(BF16))
        causal = place(iota((QT, QT), 1)) >= place(iota((QT, QT), 0))
        for m in range(TILES):
            lo, hi = m * QT, (m + 1) * QT
            k = k_ref[lo:hi, :HEAD_DIM]
            p = jnp.where(causal, jnp.exp2(dot_rows(k, qt_ref[:, lo:hi])), 0.0)
            acc_ref[:, lo:hi] += dot_rows(vt_ref[m], p.astype(BF16))
            p = jnp.exp2(dot_rows(k, qt_ref[:, hi:]))
            acc_ref[:, hi:] += dot_rows(vt_ref[m], p.astype(BF16))

    @pl.when(jnp.logical_not(safe))
    def _():
        lane = iota((QT, QUERIES), 1)
        q_at = jnp.where(lane < COUNT, lane // QT * QT + place(lane % QT), COUNT)
        k_at = place(iota((QT, QUERIES), 0))
        s = dot_rows(gk, qt_ref[...])
        top = jnp.max(s, axis=0, keepdims=True)
        acc_ref[...] = dot_rows(gvt, jnp.exp2(s - top).astype(BF16))

        def body(m, top):
            at = pl.multiple_of(m * QT, QT)
            s = dot_rows(k_ref[pl.ds(at, QT), :][:, :HEAD_DIM], qt_ref[...])
            key = k_at + m * QT
            s = jnp.where((key <= q_at) & (key < valid), s, LOW)
            new = jnp.maximum(top, jnp.max(s, axis=0, keepdims=True))
            p = jnp.exp2(s - new).astype(BF16)
            acc_ref[...] = acc_ref[...] * jnp.exp2(top - new) + dot_rows(vt_ref[m], p)
            return new

        lax.fori_loop(0, TILES, body, top)

    acc = acc_ref[...]
    o = acc[:HEAD_DIM] / acc[HEAD_DIM : HEAD_DIM + 1]
    glob_ref[...] = o[:, COUNT:].T.astype(BF16)
    for t in range(2):
        bands = []
        for j in range(4):
            at = (t * 4 + j) * PR
            bands.append(
                jnp.concatenate([o[:, n * QT + at : n * QT + at + PR] for n in range(TILES)], axis=1)
            )
        packed = jnp.concatenate(bands, axis=0).T.astype(BF16)
        att_ref[:, :, t * 128 : (t + 1) * 128] = packed.reshape(DEVICES, 2, 128)


def attend_call(lengths, recv):
    vmem = pl.BlockSpec(memory_space=pltpu.VMEM)
    return pl.pallas_call(
        attend_kernel,
        in_specs=[pl.BlockSpec(memory_space=pltpu.SMEM), vmem],
        out_specs=[vmem, vmem],
        out_shape=[
            jax.ShapeDtypeStruct((DEVICES, 2, 256), BF16),
            jax.ShapeDtypeStruct((GLOBALS, HEAD_DIM), BF16),
        ],
        scratch_shapes=[
            pltpu.VMEM((HEAD_DIM, QUERIES), BF16),
            pltpu.VMEM((COUNT, 128), BF16),
            pltpu.VMEM((TILES, VROWS, QT), BF16),
            pltpu.VMEM((512, 128), F32),
            pltpu.VMEM((VROWS, QUERIES), F32),
        ],
        compiler_params=pltpu.CompilerParams(vmem_limit_bytes=56 * 2**20),
        name="attend",
    )(lengths, recv)


def output_kernel(back_ref, merged_ref, mixed_out_ref, out_ref, wide_ref, sum_ref):
    for h in range(HEADS):
        rows = mixed_out_ref[h * HEAD_DIM : (h + 1) * HEAD_DIM, :]
        for j in range(4):
            wide_ref[h * 128 + j * HEAD_DIM : h * 128 + (j + 1) * HEAD_DIM, :] = rows
    block = iota((2 * USERS, 128), 1) // HEAD_DIM
    keep = [(block == j).astype(F32).astype(BF16) for j in range(4)]
    parts = [[] for _ in range(8)]
    for h in range(HEADS):
        for t in range(2):
            x = back_ref[:, h, :, t * 128 : (t + 1) * 128].reshape(2 * USERS, 128)
            for j in range(4):
                parts[t * 4 + j].append(x * keep[j])
    lhs = jnp.concatenate([jnp.concatenate(p, axis=1) for p in parts], axis=0)
    prod = dot_rows(lhs, wide_ref[...])
    for c in range(4):
        cols = slice(c * 128, (c + 1) * 128)
        for i in range(8):
            rows = slice(i * 2 * USERS, (i + 1) * 2 * USERS)
            sum_ref[c, pl.ds(i, 2 * USERS, stride=8), :] = prod[rows, cols]
        out_ref[:, cols] = (merged_ref[:, cols].astype(F32) + sum_ref[c]).astype(BF16)


def output_call(back, merged, mixed_out):
    vmem = pl.BlockSpec(memory_space=pltpu.VMEM)
    return pl.pallas_call(
        output_kernel,
        in_specs=[vmem] * 3,
        out_specs=vmem,
        out_shape=jax.ShapeDtypeStruct((USERS * TOKENS, WIDTH), BF16),
        scratch_shapes=[
            pltpu.VMEM((HEADS * 128, WIDTH), BF16),
            pltpu.VMEM((4, USERS * TOKENS, 128), F32),
        ],
        compiler_params=pltpu.CompilerParams(vmem_limit_bytes=48 * 2**20),
        name="output",
    )(back, merged, mixed_out)


def per_device(
    events,
    global_tokens,
    lengths,
    inner_qkv,
    inner_out,
    merge_gain,
    global_gain,
    mixed_qkv,
    mixed_out,
):
    merged, payload = inner_call(
        events,
        global_tokens.reshape(USERS, WIDTH),
        inner_qkv,
        inner_out,
        merge_gain.reshape(1, WIDTH),
        global_gain.reshape(1, WIDTH),
        mixed_qkv,
    )
    arrived = lax.all_to_all(
        payload.reshape(DEVICES, 2, 896), ("seq", "head"), split_axis=0, concat_axis=0, tiled=True
    )
    att, glob = attend_call(lengths, arrived)
    back = lax.all_to_all(att, ("seq", "head"), split_axis=0, concat_axis=0, tiled=True)
    out = output_call(back.reshape(USERS, HEADS, 2, 256), merged, mixed_out)
    return (out.reshape(USERS, TOKENS, WIDTH), glob.reshape(1, 1, GLOBALS * HEAD_DIM))


def solution(mesh):
    in_specs = (
        P(None, ("seq", "head"), None),
        P(None, "seq", None),
        P(),
        P(),
        P(),
        P(),
        P(),
        P(),
        P(),
    )
    out_specs = (P(None, ("seq", "head"), None), P("seq", "head", None))
    return jax.shard_map(
        per_device, mesh=mesh, in_specs=in_specs, out_specs=out_specs, check_vma=False
    )
```

time: 119 us -> 112 us (0.941)
  blocking collectives: 0 us -> 44.4 us
  waiting for transfers between devices: 39.8 us -> 13.7 us
  starting transfers between devices: 21.9 us -> 6.22 us
  local copies, waits for them, and re-layouts: 7.22 us -> 1.47 us
  between operations: 3.3 us -> 0.67 us
  Pallas kernels: 46.6 us -> 44.8 us
    all_to_all x0 -> x1, blocking collectives: none -> 44.4 us  [per_device(): lax.all_to_all(payload.reshape(DEVICES, 2, 896), ('seq', 'head'), split_a...]
    all_to_all x1 -> x0, waiting for transfers between devices: 25.4 us -> none  [per_device(): lax.all_to_all(payload.reshape(DEVICES, 2, 896), ('seq', 'head'), split_a...]
    all_to_all x1 -> x0, starting transfers between devices: 15.7 us -> none  [per_device(): lax.all_to_all(payload.reshape(DEVICES, 2, 896), ('seq', 'head'), split_a...]
    unnamed x16 -> x4, local copies, waits for them, and re-layouts: 5.94 us -> 0.01 us
    pallas_call x1, Pallas kernels: 33.5 us -> 30 us  [attend_call(): pl.pallas_call(attend_kernel, in_specs=[pl.BlockSpec(memory_space=pltpu.S...]
    pallas_call x1, Pallas kernels: 11.4 us -> 13.1 us  [inner_call(): pl.pallas_call(inner_kernel, grid=(USERS // STEP_USERS,), in_specs=[pl.Bl...]
  transfers between devices with their start and end apart: 2 -> 1, of which waited for: 2 -> 1; matrix products, arithmetic and copies ran while one was open for 1% -> 1% of each run, Pallas kernels for 0% -> 0%
where the time goes in v2:
time: 112 us; the launch traced here: 111 us
  Pallas kernels  44.8 us (40%)
  blocking collectives  44.4 us (40%)
  waiting for transfers between devices  13.7 us (12%)
  starting transfers between devices  6.22 us (6%)
  local copies, waits for them, and re-layouts  1.47 us (1%)
    all_to_all x1, blocking collectives, per_device(): lax.all_to_all(payload.reshape(DEVICES, 2, 896), ('seq', 'head'), split_a...  44.4 us
    pallas_call x1, Pallas kernels, attend_call(): pl.pallas_call(attend_kernel, in_specs=[pl.BlockSpec(memory_space=pltpu.S...  30 us
    all_to_all x1, waiting for transfers between devices, per_device(): lax.all_to_all(att, ('seq', 'head'), split_axis=0, concat_axis=0, tiled=T...  13.7 us
    pallas_call x1, Pallas kernels, inner_call(): pl.pallas_call(inner_kernel, grid=(USERS // STEP_USERS,), in_specs=[pl.Bl...  13.1 us
    all_to_all x1, starting transfers between devices, per_device(): lax.all_to_all(att, ('seq', 'head'), split_axis=0, concat_axis=0, tiled=T...  6.22 us
  transfers between devices with their start and end apart: 1, of which 1 were waited for; matrix products, arithmetic and copies ran while one was open for 1% of the time, Pallas kernels for 0%

profile of v2, /device:TPU:1, one launch (start us, length us, event | category | flops | bytes accessed | tf_op | source)
XLA Modules:
  0.0 111.2 jit_solution(17775797692077398619)
XLA Ops:
  0.6 13.1 %inner.1 = (bf16[256,512]{1,0:T(8,128)(2,1)}, bf16[16,16,2,896]{3,2,1,0:T(2,128)(2,1)}) custom-call(bf16[16,128,512]{2,1,0:T(8,128)(2,1)} %events_ref.1, bf16[16,512]{1,0:T(8,128)(2,1)} %bitcast.9, bf16[512,1536]{1,0:T(8,128)(2,1)} %inner_qkv_hbm.1, bf16[512,512]{1,0:T(8,128)(2,1)} %inner_out_hbm.1, f32[1,512]{1,0:T(1,128)} %bitcast.10, f32[1,512]{1,0:T(1,128)} %bitcast.11, ...), custom_call_target="tpu_custom_call" | custom-call | tf_op jit(solution)/shard_map/inner/pallas_call | solution.py:212
  13.8 0.0 copy-start
  13.8 0.0 copy-start.1
  13.8 44.4 %all_to_all.10.recv_ref = bf16[256,2,896]{2,1,0:T(2,128)(2,1)} all-to-all(bf16[256,2,896]{2,1,0:T(2,128)(2,1)} %bitcast.7), channel_id=1, replica_groups=mesh['seq'=128,'head'=2] {'seq','head'}, dimensions={0} | all-to-all | bytes 1835008 | tf_op jit(solution)/shard_map/all_to_all | solution.py:425
  58.2 30.0 %attend.1 = (bf16[256,2,256]{2,1,0:T(2,128)(2,1)}, bf16[128,32]{1,0:T(8,128)(2,1)}) custom-call(s32[16]{0:T(128)} %lengths_ref.1, bf16[256,2,896]{2,1,0:T(2,128)(2,1)} %all_to_all.10.recv_ref), custom_call_target="tpu_custom_call" | custom-call | tf_op jit(solution)/shard_map/attend/pallas_call | solution.py:346
  88.2 6.2 %all-to-all-start.1 = ((bf16[256,2,256]{2,1,0:T(2,128)(2,1)}), bf16[256,2,256]{2,1,0:T(2,128)(2,1)S(1)}, u32[]{:S(2)}, u32[]{:S(2)}) async-start(bf16[256,2,256]{2,1,0:T(2,128)(2,1)} %get-tuple-element.7), calls=%async_computation.1 | async-start | bytes 524288 | tf_op jit(solution)/shard_map/all_to_all | solution.py:429
  94.4 1.5 %reshape.31 = bf16[1,1,4096]{2,1,0:T(2,128)(2,1)} reshape(bf16[128,32]{1,0:T(8,128)(2,1)} %get-tuple-element.9) | data formatting | bytes 16384 | tf_op jit(solution)/shard_map/reshape | solution.py:431
  95.9 13.7 %all-to-all-done.1 = bf16[256,2,256]{2,1,0:T(2,128)(2,1)S(1)} async-done(((bf16[256,2,256]{2,1,0:T(2,128)(2,1)}), bf16[256,2,256]{2,1,0:T(2,128)(2,1)S(1)}, u32[]{:S(2)}, u32[]{:S(2)}) %all-to-all-start.1) | async-done | bytes 262176 | tf_op jit(solution)/shard_map/all_to_all | solution.py:429
  109.5 0.0 copy-done
  109.5 0.0 copy-done.1
  109.5 1.7 %output.1 = bf16[256,512]{1,0:T(8,128)(2,1)} custom-call(bf16[16,16,2,256]{3,2,1,0:T(2,128)(2,1)S(1)} %bitcast.6, bf16[256,512]{1,0:T(8,128)(2,1)S(1)} %copy-done.1, bf16[512,512]{1,0:T(8,128)(2,1)S(1)} %copy-done), custom_call_target="tpu_custom_call" | custom-call | tf_op jit(solution)/shard_map/output/pallas_call | solution.py:391
Async XLA Ops:
  13.8 95.8 %copy-start = (bf16[512,512]{1,0:T(8,128)(2,1)S(1)}, bf16[512,512]{1,0:T(8,128)(2,1)}, u32[]{:S(2)}) copy-start(bf16[512,512]{1,0:T(8,128)(2,1)} %mixed_out_ref.1) | copy-start | bytes 1572868
  13.8 95.8 %copy-start.1 = (bf16[256,512]{1,0:T(8,128)(2,1)S(1)}, bf16[256,512]{1,0:T(8,128)(2,1)}, u32[]{:S(2)}) copy-start(bf16[256,512]{1,0:T(8,128)(2,1)} %get-tuple-element.8.merged_ref) | copy-start | bytes 786436
  88.2 21.4 %all-to-all-start.1 = ((bf16[256,2,256]{2,1,0:T(2,128)(2,1)}), bf16[256,2,256]{2,1,0:T(2,128)(2,1)S(1)}, u32[]{:S(2)}, u32[]{:S(2)}) async-start(bf16[256,2,256]{2,1,0:T(2,128)(2,1)} %get-tuple-element.7), calls=%async_computation.1 | async-start | bytes 524288 | tf_op jit(solution)/shard_map/all_to_all | solution.py:429

commit v3 on v2

--- a/solution.py
+++ b/solution.py
@@ -19,7 +19,8 @@
 TOKENS = 16
 DEVICES = 256
 COUNT = DEVICES * TOKENS
-STEP_USERS = 4
+STEP_USERS = 8
+STEPS = USERS // STEP_USERS
 SCORE_SCALE = math.log2(math.e) / math.sqrt(HEAD_DIM)
 SAFE = 100.0
 LOW = -1e30
@@ -43,7 +44,7 @@
 
 
 def inner_kernel(
-    events_ref,
+    events_hbm,
     tokens_hbm,
     inner_qkv_hbm,
     inner_out_hbm,
@@ -53,6 +54,7 @@
     merged_ref,
     payload_ref,
     normed_ref,
+    events_ref,
     tokens_ref,
     inner_qkv_ref,
     inner_out_ref,
@@ -61,11 +63,13 @@
     mixed_qkv_ref,
     sems,
 ):
-    step = pl.program_id(0)
-    fetch = []
+    fetch = [(events_hbm.at[0:STEP_USERS], events_ref.at[0:STEP_USERS])]
     for c in range(3):
         cols = slice(c * WIDTH, (c + 1) * WIDTH)
         fetch.append((inner_qkv_hbm.at[:, cols], inner_qkv_ref.at[:, cols]))
+    for n in range(1, STEPS):
+        users = slice(n * STEP_USERS, (n + 1) * STEP_USERS)
+        fetch.append((events_hbm.at[users], events_ref.at[users]))
     fetch.append((inner_out_hbm, inner_out_ref))
     fetch.append((merge_gain_hbm, merge_gain_ref))
     for c in range(3):
@@ -76,164 +80,163 @@
     copies = [
         pltpu.make_async_copy(src, dst, sems.at[n]) for n, (src, dst) in enumerate(fetch)
     ]
-
-    @pl.when(step == 0)
-    def _():
-        for copy in copies:
-            copy.start()
-        for copy in copies[:3]:
-            copy.wait()
-
-    x = events_ref[...].reshape(STEP_USERS * SPAN, WIDTH)
-    qkv = dot_rows(x, inner_qkv_ref[...]).astype(BF16)
+    for copy in copies:
+        copy.start()
+
     lane = iota((SPAN, 128), 1)
     low = (lane < 64).astype(F32).astype(BF16)
     high = (lane >= 64).astype(F32).astype(BF16)
     lane_group8 = iota((8, 128), 1) // 8
-    compact = []
-    for b in range(STEP_USERS):
-        rows = slice(b * SPAN, (b + 1) * SPAN)
-        for t in range(4):
-            q = qkv[rows, t * 128 : (t + 1) * 128]
-            k = qkv[rows, 512 + t * 128 : 512 + (t + 1) * 128]
-            scores = dot_last(k, jnp.concatenate([q * low, q * high], axis=0))
-            for half in range(2):
-                part = scores[:, half * 128 : (half + 1) * 128]
-                picked = part[0:8]
-                for g in range(1, TOKENS):
-                    picked = jnp.where(lane_group8 == g, part[g * 8 : g * 8 + 8], picked)
-                compact.append(picked)
-    sc = jnp.stack(compact, axis=0)
-    top = jnp.max(sc, axis=1, keepdims=True)
-    expd = jnp.exp((sc - top) * 0.125)
-    w = expd / jnp.sum(expd, axis=1, keepdims=True)
-    w = w.reshape(STEP_USERS * 64, 128)
-    same = (iota((128, 128), 0) // 8 == iota((128, 128), 1) // 8).astype(BF16)
-    w_hi = w.astype(BF16)
-    w_lo = (w - w_hi.astype(F32)).astype(BF16)
-    wm = (dot_rows(w_hi, same) + dot_rows(w_lo, same)) * 0.125
-    wm = wm.reshape(STEP_USERS * 8, 8, 128)
-    on_diag = iota((8, 128), 0) == iota((8, 128), 1) % 8
-    row = jnp.sum(jnp.where(on_diag[None], wm, 0.0), axis=1, keepdims=True)
-    group_of_lane = iota((TOKENS, 128), 1) // 8 == iota((TOKENS, 128), 0)
-    spread = jnp.where(group_of_lane[None], row, 0.0).astype(BF16)
-    mean_w = jnp.where(group_of_lane, 0.125, 0.0).astype(BF16)
-    low_half = iota((TOKENS, 128), 1) < 64
-    pooled, means = [], []
-    for b in range(STEP_USERS):
-        rows = slice(b * SPAN, (b + 1) * SPAN)
-        tiles = []
-        for tp in range(2):
-            a = spread[b * 8 + 4 * tp : b * 8 + 4 * tp + 4].reshape(4 * TOKENS, 128)
-            r = dot_rows(a, qkv[rows, 1024 + tp * 256 : 1024 + (tp + 1) * 256])
-            for t in range(2):
-                cols = slice(t * 128, (t + 1) * 128)
-                at = 2 * t * TOKENS
-                tiles.append(
-                    jnp.where(low_half, r[at : at + TOKENS, cols], r[at + TOKENS : at + 2 * TOKENS, cols])
-                )
-        pooled.append(jnp.concatenate(tiles, axis=1))
-        means.append(dot_rows(mean_w, x[rows]))
-    pooled = jnp.concatenate(pooled, axis=0).astype(BF16)
-
-    @pl.when(step == 0)
-    def _():
-        for copy in copies[3:5]:
+
+    def project(step):
+        for copy in copies[:4] if step == 0 else copies[3 + step : 4 + step]:
             copy.wait()
-
-    merged = jnp.concatenate(means, axis=0) + dot_rows(pooled, inner_out_ref[...])
-    merged = merged.astype(BF16)
-    merged_ref[...] = merged
-    rows = STEP_USERS * TOKENS
-    normed = norm_f32(merged.astype(F32), merge_gain_ref[...])
-    for c in range(4):
-        normed_ref[c, pl.ds(pl.multiple_of(step * rows, rows), rows), :] = normed[
-            :, c * 128 : (c + 1) * 128
-        ]
-
-    @pl.when(step == USERS // STEP_USERS - 1)
-    def _():
-        for copy in copies[5:]:
-            copy.wait()
-        slab_rows = jnp.concatenate(
-            [
-                jnp.concatenate(
-                    [normed_ref[c, pl.ds(i, 2 * USERS, stride=8), :] for i in range(8)], axis=0
-                ).astype(BF16)
-                for c in range(4)
-            ],
-            axis=1,
-        )
-        lane_block = iota((2 * USERS, 128), 1) // HEAD_DIM
-        for c in range(3):
-            for hp in range(2):
-                col = c * 512 + hp * 256
-                pair = dot_rows(slab_rows, mixed_qkv_ref[:, col : col + 256])
-                if c == 0:
-                    pair = pair * SCORE_SCALE
-                for ht in (2 * hp, 2 * hp + 1):
-                    part = pair[:, (ht % 2) * 128 : (ht % 2 + 1) * 128]
-                    for t in range(2):
-                        base = [
-                            part[(t * 4 + j) * 2 * USERS : (t * 4 + j + 1) * 2 * USERS]
-                            for j in range(4)
-                        ]
-                        for hh in range(4):
-                            out = None
-                            for j in range(4):
-                                shift = (HEAD_DIM * (j - hh)) % 128
-                                moved = pltpu.roll(base[j], shift, 1) if shift else base[j]
-                                out = moved if j == 0 else jnp.where(lane_block == j, moved, out)
-                            tile = (c * 2 + t) * 128
-                            payload_ref[:, ht * 4 + hh, :, tile : tile + 128] = out.astype(
-                                BF16
-                            ).reshape(USERS, 2, 128)
-        gnormed = norm_f32(tokens_ref[...].astype(F32), global_gain_ref[...]).astype(BF16)
-        block16 = iota((USERS, 128), 1) // HEAD_DIM
-        gqkv = [
-            dot_rows(gnormed, mixed_qkv_ref[:, c * 512 : (c + 1) * 512]) for c in range(3)
-        ]
-        gqkv[0] = gqkv[0] * SCORE_SCALE
-        for ht in range(4):
-            sect = [part[:, ht * 128 : (ht + 1) * 128] for part in gqkv]
-            for hh in range(4):
-                out = jnp.zeros((USERS, 128), F32)
-                for c in range(3):
-                    shift = (HEAD_DIM * (c - hh)) % 128
-                    moved = pltpu.roll(sect[c], shift, 1) if shift else sect[c]
-                    out = jnp.where(block16 == c, moved, out)
-                payload_ref[:, ht * 4 + hh, :, 768:896] = jnp.broadcast_to(
-                    out[:, None, :], (USERS, 2, 128)
-                ).astype(BF16)
+        x = events_ref[step * STEP_USERS : (step + 1) * STEP_USERS]
+        x = x.reshape(STEP_USERS * SPAN, WIDTH)
+        return x, dot_rows(x, inner_qkv_ref[...]).astype(BF16)
+
+    def merge(step, x, qkv):
+        compact = []
+        for b in range(STEP_USERS):
+            rows = slice(b * SPAN, (b + 1) * SPAN)
+            for t in range(4):
+                q = qkv[rows, t * 128 : (t + 1) * 128]
+                k = qkv[rows, 512 + t * 128 : 512 + (t + 1) * 128]
+                scores = dot_last(k, jnp.concatenate([q * low, q * high], axis=0))
+                for half in range(2):
+                    part = scores[:, half * 128 : (half + 1) * 128]
+                    picked = part[0:8]
+                    for g in range(1, TOKENS):
+                        picked = jnp.where(lane_group8 == g, part[g * 8 : g * 8 + 8], picked)
+                    compact.append(picked)
+        sc = jnp.stack(compact, axis=0)
+        top = jnp.max(sc, axis=1, keepdims=True)
+        expd = jnp.exp((sc - top) * 0.125)
+        w = expd / jnp.sum(expd, axis=1, keepdims=True)
+        w = w.reshape(STEP_USERS * 64, 128)
+        same = (iota((128, 128), 0) // 8 == iota((128, 128), 1) // 8).astype(BF16)
+        w_hi = w.astype(BF16)
+        w_lo = (w - w_hi.astype(F32)).astype(BF16)
+        wm = (dot_rows(w_hi, same) + dot_rows(w_lo, same)) * 0.125
+        wm = wm.reshape(STEP_USERS * 8, 8, 128)
+        on_diag = iota((8, 128), 0) == iota((8, 128), 1) % 8
+        row = jnp.sum(jnp.where(on_diag[None], wm, 0.0), axis=1, keepdims=True)
+        group_of_lane = iota((TOKENS, 128), 1) // 8 == iota((TOKENS, 128), 0)
+        spread = jnp.where(group_of_lane[None], row, 0.0).astype(BF16)
+        mean_w = jnp.where(group_of_lane, 0.125, 0.0).astype(BF16)
+        low_half = iota((TOKENS, 128), 1) < 64
+        pooled, means = [], []
+        for b in range(STEP_USERS):
+            rows = slice(b * SPAN, (b + 1) * SPAN)
+            tiles = []
+            for tp in range(2):
+                a = spread[b * 8 + 4 * tp : b * 8 + 4 * tp + 4].reshape(4 * TOKENS, 128)
+                r = dot_rows(a, qkv[rows, 1024 + tp * 256 : 1024 + (tp + 1) * 256])
+                for t in range(2):
+                    cols = slice(t * 128, (t + 1) * 128)
+                    at = 2 * t * TOKENS
+                    tiles.append(
+                        jnp.where(low_half, r[at : at + TOKENS, cols], r[at + TOKENS : at + 2 * TOKENS, cols])
+                    )
+            pooled.append(jnp.concatenate(tiles, axis=1))
+            means.append(dot_rows(mean_w, x[rows]))
+        pooled = jnp.concatenate(pooled, axis=0).astype(BF16)
+
+        if step == 0:
+            copies[3 + STEPS].wait()
+            copies[4 + STEPS].wait()
+        merged = jnp.concatenate(means, axis=0) + dot_rows(pooled, inner_out_ref[...])
+        merged = merged.astype(BF16)
+        rows = STEP_USERS * TOKENS
+        merged_ref[step * rows : (step + 1) * rows, :] = merged
+        normed = norm_f32(merged.astype(F32), merge_gain_ref[...])
+        for c in range(4):
+            normed_ref[c, step * rows : (step + 1) * rows, :] = normed[:, c * 128 : (c + 1) * 128]
+
+    ahead = project(0)
+    for step in range(STEPS):
+        x, qkv = ahead
+        if step + 1 < STEPS:
+            ahead = project(step + 1)
+        merge(step, x, qkv)
+
+    for copy in copies[5 + STEPS :]:
+        copy.wait()
+    slab_rows = jnp.concatenate(
+        [
+            jnp.concatenate(
+                [normed_ref[c, pl.ds(i, 2 * USERS, stride=8), :] for i in range(8)], axis=0
+            ).astype(BF16)
+            for c in range(4)
+        ],
+        axis=1,
+    )
+    lane_block = iota((2 * USERS, 128), 1) // HEAD_DIM
+    for c in range(3):
+        for hp in range(2):
+            col = c * 512 + hp * 256
+            pair = dot_rows(slab_rows, mixed_qkv_ref[:, col : col + 256])
+            if c == 0:
+                pair = pair * SCORE_SCALE
+            for ht in (2 * hp, 2 * hp + 1):
+                part = pair[:, (ht % 2) * 128 : (ht % 2 + 1) * 128]
+                for t in range(2):
+                    base = [
+                        part[(t * 4 + j) * 2 * USERS : (t * 4 + j + 1) * 2 * USERS]
+                        for j in range(4)
+                    ]
+                    for hh in range(4):
+                        out = None
+                        for j in range(4):
+                            shift = (HEAD_DIM * (j - hh)) % 128
+                            moved = pltpu.roll(base[j], shift, 1) if shift else base[j]
+                            out = moved if j == 0 else jnp.where(lane_block == j, moved, out)
+                        tile = (c * 2 + t) * 128
+                        payload_ref[:, ht * 4 + hh, :, tile : tile + 128] = out.astype(
+                            BF16
+                        ).reshape(USERS, 2, 128)
+    gnormed = norm_f32(tokens_ref[...].astype(F32), global_gain_ref[...]).astype(BF16)
+    block16 = iota((USERS, 128), 1) // HEAD_DIM
+    gqkv = [
+        dot_rows(gnormed, mixed_qkv_ref[:, c * 512 : (c + 1) * 512]) for c in range(3)
+    ]
+    gqkv[0] = gqkv[0] * SCORE_SCALE
+    for ht in range(4):
+        sect = [part[:, ht * 128 : (ht + 1) * 128] for part in gqkv]
+        for hh in range(4):
+            out = jnp.zeros((USERS, 128), F32)
+            for c in range(3):
+                shift = (HEAD_DIM * (c - hh)) % 128
+                moved = pltpu.roll(sect[c], shift, 1) if shift else sect[c]
+                out = jnp.where(block16 == c, moved, out)
+            payload_ref[:, ht * 4 + hh, :, 768:896] = jnp.broadcast_to(
+                out[:, None, :], (USERS, 2, 128)
+            ).astype(BF16)
 
 
 def inner_call(events, tokens, inner_qkv, inner_out, merge_gain, global_gain, mixed_qkv):
     hbm = pl.BlockSpec(memory_space=pl.ANY)
+    vmem = pl.BlockSpec(memory_space=pltpu.VMEM)
     return pl.pallas_call(
         inner_kernel,
-        grid=(USERS // STEP_USERS,),
-        in_specs=[pl.BlockSpec((STEP_USERS, SPAN, WIDTH), lambda i: (i, 0, 0))] + [hbm] * 6,
-        out_specs=[
-            pl.BlockSpec((STEP_USERS * TOKENS, WIDTH), lambda i: (i, 0)),
-            pl.BlockSpec((USERS, HEADS, 2, 896), lambda i: (0, 0, 0, 0)),
-        ],
+        in_specs=[hbm] * 7,
+        out_specs=[vmem, vmem],
         out_shape=[
             jax.ShapeDtypeStruct((USERS * TOKENS, WIDTH), BF16),
             jax.ShapeDtypeStruct((USERS, HEADS, 2, 896), BF16),
         ],
         scratch_shapes=[
             pltpu.VMEM((4, USERS * TOKENS, 128), F32),
+            pltpu.VMEM((USERS, SPAN, WIDTH), BF16),
             pltpu.VMEM((USERS, WIDTH), BF16),
             pltpu.VMEM((WIDTH, 3 * WIDTH), BF16),
             pltpu.VMEM((WIDTH, WIDTH), BF16),
             pltpu.VMEM((1, WIDTH), F32),
             pltpu.VMEM((1, WIDTH), F32),
             pltpu.VMEM((WIDTH, 3 * WIDTH), BF16),
-            pltpu.SemaphoreType.DMA((10,)),
-        ],
-        compiler_params=pltpu.CompilerParams(
-            dimension_semantics=("arbitrary",), vmem_limit_bytes=60 * 2**20
-        ),
+            pltpu.SemaphoreType.DMA((STEPS + 10,)),
+        ],
+        compiler_params=pltpu.CompilerParams(vmem_limit_bytes=60 * 2**20),
         name="inner",
     )(events, tokens, inner_qkv, inner_out, merge_gain, global_gain, mixed_qkv)
 

time: 112 us -> 109 us (0.973)
  Pallas kernels: 44.8 us -> 42.4 us
    pallas_call x1, Pallas kernels: 13.1 us -> 10.7 us  [inner_call(): pl.pallas_call(inner_kernel, in_specs=[hbm] * 7, out_specs=[vmem, vmem],...]
where the time goes in v3:
time: 109 us
  blocking collectives  44.4 us (41%)
  Pallas kernels  42.4 us (39%)
  waiting for transfers between devices  13.7 us (13%)
  starting transfers between devices  6.23 us (6%)
  local copies, waits for them, and re-layouts  1.47 us (1%)
    all_to_all x1, blocking collectives, per_device(): lax.all_to_all(payload.reshape(DEVICES, 2, 896), ('seq', 'head'), split_a...  44.4 us
    pallas_call x1, Pallas kernels, attend_call(): pl.pallas_call(attend_kernel, in_specs=[pl.BlockSpec(memory_space=pltpu.S...  30 us
    all_to_all x1, waiting for transfers between devices, per_device(): lax.all_to_all(att, ('seq', 'head'), split_axis=0, concat_axis=0, tiled=T...  13.7 us
    pallas_call x1, Pallas kernels, inner_call(): pl.pallas_call(inner_kernel, in_specs=[hbm] * 7, out_specs=[vmem, vmem],...  10.7 us
    all_to_all x1, starting transfers between devices, per_device(): lax.all_to_all(att, ('seq', 'head'), split_axis=0, concat_axis=0, tiled=T...  6.23 us
  transfers between devices with their start and end apart: 1, of which 1 were waited for; matrix products, arithmetic and copies ran while one was open for 1% of the time, Pallas kernels for 0%

profile of v3, /device:TPU:1, one launch (start us, length us, event | category | flops | bytes accessed | tf_op | source)
XLA Modules:
  0.0 108.8 jit_solution(18071401514477861049)
XLA Ops:
  0.6 10.7 %inner.1 = (bf16[256,512]{1,0:T(8,128)(2,1)}, bf16[16,16,2,896]{3,2,1,0:T(2,128)(2,1)}) custom-call(bf16[16,128,512]{2,1,0:T(8,128)(2,1)} %events_hbm.1, bf16[16,512]{1,0:T(8,128)(2,1)} %bitcast.9, bf16[512,1536]{1,0:T(8,128)(2,1)} %inner_qkv_hbm.1, bf16[512,512]{1,0:T(8,128)(2,1)} %inner_out_hbm.1, f32[1,512]{1,0:T(1,128)} %bitcast.10, f32[1,512]{1,0:T(1,128)} %bitcast.11, ...), custom_call_target="tpu_custom_call" | custom-call | tf_op jit(solution)/shard_map/inner/pallas_call | solution.py:220
  11.3 0.0 copy-start
  11.3 0.0 copy-start.1
  11.3 44.4 %all_to_all.10.recv_ref = bf16[256,2,896]{2,1,0:T(2,128)(2,1)} all-to-all(bf16[256,2,896]{2,1,0:T(2,128)(2,1)} %bitcast.7), channel_id=1, replica_groups=mesh['seq'=128,'head'=2] {'seq','head'}, dimensions={0} | all-to-all | bytes 1835008 | tf_op jit(solution)/shard_map/all_to_all | solution.py:428
  55.7 30.0 %attend.1 = (bf16[256,2,256]{2,1,0:T(2,128)(2,1)}, bf16[128,32]{1,0:T(8,128)(2,1)}) custom-call(s32[16]{0:T(128)} %lengths_ref.1, bf16[256,2,896]{2,1,0:T(2,128)(2,1)} %all_to_all.10.recv_ref), custom_call_target="tpu_custom_call" | custom-call | tf_op jit(solution)/shard_map/attend/pallas_call | solution.py:349
  85.7 6.2 %all-to-all-start.1 = ((bf16[256,2,256]{2,1,0:T(2,128)(2,1)}), bf16[256,2,256]{2,1,0:T(2,128)(2,1)S(1)}, u32[]{:S(2)}, u32[]{:S(2)}) async-start(bf16[256,2,256]{2,1,0:T(2,128)(2,1)} %get-tuple-element.7), calls=%async_computation.1 | async-start | bytes 524288 | tf_op jit(solution)/shard_map/all_to_all | solution.py:432
  92.0 1.5 %reshape.31 = bf16[1,1,4096]{2,1,0:T(2,128)(2,1)} reshape(bf16[128,32]{1,0:T(8,128)(2,1)} %get-tuple-element.9) | data formatting | bytes 16384 | tf_op jit(solution)/shard_map/reshape | solution.py:434
  93.4 13.7 %all-to-all-done.1 = bf16[256,2,256]{2,1,0:T(2,128)(2,1)S(1)} async-done(((bf16[256,2,256]{2,1,0:T(2,128)(2,1)}), bf16[256,2,256]{2,1,0:T(2,128)(2,1)S(1)}, u32[]{:S(2)}, u32[]{:S(2)}) %all-to-all-start.1) | async-done | bytes 262176 | tf_op jit(solution)/shard_map/all_to_all | solution.py:432
  107.1 0.0 copy-done
  107.1 0.0 copy-done.1
  107.1 1.7 %output.1 = bf16[256,512]{1,0:T(8,128)(2,1)} custom-call(bf16[16,16,2,256]{3,2,1,0:T(2,128)(2,1)S(1)} %bitcast.6, bf16[256,512]{1,0:T(8,128)(2,1)S(1)} %copy-done.1, bf16[512,512]{1,0:T(8,128)(2,1)S(1)} %copy-done), custom_call_target="tpu_custom_call" | custom-call | tf_op jit(solution)/shard_map/output/pallas_call | solution.py:394
Async XLA Ops:
  11.3 95.8 %copy-start = (bf16[512,512]{1,0:T(8,128)(2,1)S(1)}, bf16[512,512]{1,0:T(8,128)(2,1)}, u32[]{:S(2)}) copy-start(bf16[512,512]{1,0:T(8,128)(2,1)} %mixed_out_ref.1) | copy-start | bytes 1572868
  11.3 95.8 %copy-start.1 = (bf16[256,512]{1,0:T(8,128)(2,1)S(1)}, bf16[256,512]{1,0:T(8,128)(2,1)}, u32[]{:S(2)}) copy-start(bf16[256,512]{1,0:T(8,128)(2,1)} %get-tuple-element.8.merged_ref) | copy-start | bytes 786436
  85.7 21.4 %all-to-all-start.1 = ((bf16[256,2,256]{2,1,0:T(2,128)(2,1)}), bf16[256,2,256]{2,1,0:T(2,128)(2,1)S(1)}, u32[]{:S(2)}, u32[]{:S(2)}) async-start(bf16[256,2,256]{2,1,0:T(2,128)(2,1)} %get-tuple-element.7), calls=%async_computation.1 | async-start | bytes 524288 | tf_op jit(solution)/shard_map/all_to_all | solution.py:432

commit v4 on v3

--- a/solution.py
+++ b/solution.py
@@ -80,7 +80,7 @@
     copies = [
         pltpu.make_async_copy(src, dst, sems.at[n]) for n, (src, dst) in enumerate(fetch)
     ]
-    for copy in copies:
+    for copy in copies[:4]:
         copy.start()
 
     lane = iota((SPAN, 128), 1)
@@ -91,6 +91,9 @@
     def project(step):
         for copy in copies[:4] if step == 0 else copies[3 + step : 4 + step]:
             copy.wait()
+        if step == 0:
+            for copy in copies[4:]:
+                copy.start()
         x = events_ref[step * STEP_USERS : (step + 1) * STEP_USERS]
         x = x.reshape(STEP_USERS * SPAN, WIDTH)
         return x, dot_rows(x, inner_qkv_ref[...]).astype(BF16)
@@ -361,7 +364,7 @@
             pltpu.VMEM((512, 128), F32),
             pltpu.VMEM((VROWS, QUERIES), F32),
         ],
-        compiler_params=pltpu.CompilerParams(vmem_limit_bytes=56 * 2**20),
+        compiler_params=pltpu.CompilerParams(vmem_limit_bytes=32 * 2**20),
         name="attend",
     )(lengths, recv)
 
@@ -400,7 +403,7 @@
             pltpu.VMEM((HEADS * 128, WIDTH), BF16),
             pltpu.VMEM((4, USERS * TOKENS, 128), F32),
         ],
-        compiler_params=pltpu.CompilerParams(vmem_limit_bytes=48 * 2**20),
+        compiler_params=pltpu.CompilerParams(vmem_limit_bytes=16 * 2**20),
         name="output",
     )(back, merged, mixed_out)
 

time: 109 us -> 108 us (level)
  no operation moved by 1% of the time
where the time goes in v4:
time: 108 us
  blocking collectives  44.3 us (41%)
  Pallas kernels  41.7 us (39%)
  waiting for transfers between devices  14.4 us (13%)
  starting transfers between devices  6.23 us (6%)
    all_to_all x1, blocking collectives, per_device(): lax.all_to_all(payload.reshape(DEVICES, 2, 896), ('seq', 'head'), split_a...  44.3 us
    pallas_call x1, Pallas kernels, attend_call(): pl.pallas_call(attend_kernel, in_specs=[pl.BlockSpec(memory_space=pltpu.S...  29.4 us
    all_to_all x1, waiting for transfers between devices, per_device(): lax.all_to_all(att, ('seq', 'head'), split_axis=0, concat_axis=0, tiled=T...  14.4 us
    pallas_call x1, Pallas kernels, inner_call(): pl.pallas_call(inner_kernel, in_specs=[hbm] * 7, out_specs=[vmem, vmem],...  10.6 us
    all_to_all x1, starting transfers between devices, per_device(): lax.all_to_all(att, ('seq', 'head'), split_axis=0, concat_axis=0, tiled=T...  6.23 us
  transfers between devices with their start and end apart: 1, of which 1 were waited for; matrix products, arithmetic and copies ran while one was open for 1% of the time, Pallas kernels for 0%

profile of v4, /device:TPU:1, one launch (start us, length us, event | category | flops | bytes accessed | tf_op | source)
XLA Modules:
  0.0 108.0 jit_solution(10474254365711538830)
XLA Ops:
  0.6 10.6 %inner.1 = (bf16[256,512]{1,0:T(8,128)(2,1)}, bf16[16,16,2,896]{3,2,1,0:T(2,128)(2,1)}) custom-call(bf16[16,128,512]{2,1,0:T(8,128)(2,1)} %events_hbm.1, bf16[16,512]{1,0:T(8,128)(2,1)} %bitcast.9, bf16[512,1536]{1,0:T(8,128)(2,1)} %inner_qkv_hbm.1, bf16[512,512]{1,0:T(8,128)(2,1)} %inner_out_hbm.1, f32[1,512]{1,0:T(1,128)} %bitcast.10, f32[1,512]{1,0:T(1,128)} %bitcast.11, ...), custom_call_target="tpu_custom_call" | custom-call | tf_op jit(solution)/shard_map/inner/pallas_call | solution.py:223
  11.3 0.0 copy-start.2
  11.3 0.0 copy-start
  11.3 0.0 copy-start.1
  11.3 44.3 %all_to_all.10.recv_ref = bf16[256,2,896]{2,1,0:T(2,128)(2,1)S(1)} all-to-all(bf16[256,2,896]{2,1,0:T(2,128)(2,1)} %bitcast.7), channel_id=1, replica_groups=mesh['seq'=128,'head'=2] {'seq','head'}, dimensions={0} | all-to-all | bytes 1835008 | tf_op jit(solution)/shard_map/all_to_all | solution.py:431
  55.6 0.0 copy-done.2
  55.6 29.4 %attend.1 = (bf16[256,2,256]{2,1,0:T(2,128)(2,1)}, bf16[128,32]{1,0:T(8,128)(2,1)S(1)}) custom-call(s32[16]{0:T(128)S(1)} %copy-done.2, bf16[256,2,896]{2,1,0:T(2,128)(2,1)S(1)} %all_to_all.10.recv_ref), custom_call_target="tpu_custom_call" | custom-call | tf_op jit(solution)/shard_map/attend/pallas_call | solution.py:352
  85.0 6.2 %all-to-all-start.1 = ((bf16[256,2,256]{2,1,0:T(2,128)(2,1)}), bf16[256,2,256]{2,1,0:T(2,128)(2,1)S(1)}, u32[]{:S(2)}, u32[]{:S(2)}) async-start(bf16[256,2,256]{2,1,0:T(2,128)(2,1)} %get-tuple-element.7), calls=%async_computation.1 | async-start | bytes 524288 | tf_op jit(solution)/shard_map/all_to_all | solution.py:435
  91.2 0.7 reshape.31
  91.9 14.4 %all-to-all-done.1 = bf16[256,2,256]{2,1,0:T(2,128)(2,1)S(1)} async-done(((bf16[256,2,256]{2,1,0:T(2,128)(2,1)}), bf16[256,2,256]{2,1,0:T(2,128)(2,1)S(1)}, u32[]{:S(2)}, u32[]{:S(2)}) %all-to-all-start.1) | async-done | bytes 262176 | tf_op jit(solution)/shard_map/all_to_all | solution.py:435
  106.3 0.0 copy-done
  106.3 0.0 copy-done.1
  106.3 1.7 %output.1 = bf16[256,512]{1,0:T(8,128)(2,1)} custom-call(bf16[16,16,2,256]{3,2,1,0:T(2,128)(2,1)S(1)} %bitcast.6, bf16[256,512]{1,0:T(8,128)(2,1)S(1)} %copy-done.1, bf16[512,512]{1,0:T(8,128)(2,1)S(1)} %copy-done), custom_call_target="tpu_custom_call" | custom-call | tf_op jit(solution)/shard_map/output/pallas_call | solution.py:397
Async XLA Ops:
  11.3 44.3 %copy-start.2 = (s32[16]{0:T(128)S(1)}, s32[16]{0:T(128)}, u32[]{:S(2)}) copy-start(s32[16]{0:T(128)} %lengths_ref.1) | copy-start | bytes 196
  11.3 95.0 %copy-start = (bf16[512,512]{1,0:T(8,128)(2,1)S(1)}, bf16[512,512]{1,0:T(8,128)(2,1)}, u32[]{:S(2)}) copy-start(bf16[512,512]{1,0:T(8,128)(2,1)} %mixed_out_ref.1) | copy-start | bytes 1572868
  11.3 95.0 %copy-start.1 = (bf16[256,512]{1,0:T(8,128)(2,1)S(1)}, bf16[256,512]{1,0:T(8,128)(2,1)}, u32[]{:S(2)}) copy-start(bf16[256,512]{1,0:T(8,128)(2,1)} %get-tuple-element.8.merged_ref) | copy-start | bytes 786436
  85.0 21.4 %all-to-all-start.1 = ((bf16[256,2,256]{2,1,0:T(2,128)(2,1)}), bf16[256,2,256]{2,1,0:T(2,128)(2,1)S(1)}, u32[]{:S(2)}, u32[]{:S(2)}) async-start(bf16[256,2,256]{2,1,0:T(2,128)(2,1)} %get-tuple-element.7), calls=%async_computation.1 | async-start | bytes 524288 | tf_op jit(solution)/shard_map/all_to_all | solution.py:435

commit v5 on v4

--- a/solution.py
+++ b/solution.py
@@ -89,16 +89,16 @@
     lane_group8 = iota((8, 128), 1) // 8
 
     def project(step):
-        for copy in copies[:4] if step == 0 else copies[3 + step : 4 + step]:
-            copy.wait()
         if step == 0:
+            for copy in copies[:4]:
+                copy.wait()
             for copy in copies[4:]:
                 copy.start()
         x = events_ref[step * STEP_USERS : (step + 1) * STEP_USERS]
         x = x.reshape(STEP_USERS * SPAN, WIDTH)
         return x, dot_rows(x, inner_qkv_ref[...]).astype(BF16)
 
-    def merge(step, x, qkv):
+    def score(qkv):
         compact = []
         for b in range(STEP_USERS):
             rows = slice(b * SPAN, (b + 1) * SPAN)
@@ -112,7 +112,9 @@
                     for g in range(1, TOKENS):
                         picked = jnp.where(lane_group8 == g, part[g * 8 : g * 8 + 8], picked)
                     compact.append(picked)
-        sc = jnp.stack(compact, axis=0)
+        return jnp.stack(compact, axis=0)
+
+    def pool_weights(sc):
         top = jnp.max(sc, axis=1, keepdims=True)
         expd = jnp.exp((sc - top) * 0.125)
         w = expd / jnp.sum(expd, axis=1, keepdims=True)
@@ -125,7 +127,10 @@
         on_diag = iota((8, 128), 0) == iota((8, 128), 1) % 8
         row = jnp.sum(jnp.where(on_diag[None], wm, 0.0), axis=1, keepdims=True)
         group_of_lane = iota((TOKENS, 128), 1) // 8 == iota((TOKENS, 128), 0)
-        spread = jnp.where(group_of_lane[None], row, 0.0).astype(BF16)
+        return jnp.where(group_of_lane[None], row, 0.0).astype(BF16)
+
+    def merge(step, x, qkv, spread):
+        group_of_lane = iota((TOKENS, 128), 1) // 8 == iota((TOKENS, 128), 0)
         mean_w = jnp.where(group_of_lane, 0.125, 0.0).astype(BF16)
         low_half = iota((TOKENS, 128), 1) < 64
         pooled, means = [], []
@@ -145,9 +150,6 @@
             means.append(dot_rows(mean_w, x[rows]))
         pooled = jnp.concatenate(pooled, axis=0).astype(BF16)
 
-        if step == 0:
-            copies[3 + STEPS].wait()
-            copies[4 + STEPS].wait()
         merged = jnp.concatenate(means, axis=0) + dot_rows(pooled, inner_out_ref[...])
         merged = merged.astype(BF16)
         rows = STEP_USERS * TOKENS
@@ -156,12 +158,19 @@
         for c in range(4):
             normed_ref[c, step * rows : (step + 1) * rows, :] = normed[:, c * 128 : (c + 1) * 128]
 
-    ahead = project(0)
-    for step in range(STEPS):
-        x, qkv = ahead
-        if step + 1 < STEPS:
-            ahead = project(step + 1)
-        merge(step, x, qkv)
+    held, scores, spreads = {}, {}, {}
+    for turn in range(STEPS + 3):
+        if turn < STEPS:
+            held[turn] = project(turn)
+        if 0 <= turn - 1 < STEPS:
+            scores[turn - 1] = score(held[turn - 1][1])
+        if 0 <= turn - 2 < STEPS:
+            spreads[turn - 2] = pool_weights(scores[turn - 2])
+        if 0 <= turn - 3 < STEPS:
+            merge(turn - 3, *held[turn - 3], spreads[turn - 3])
+        if turn == 0:
+            for copy in copies[4 : 5 + STEPS]:
+                copy.wait()
 
     for copy in copies[5 + STEPS :]:
         copy.wait()
@@ -257,7 +266,6 @@
 
 def attend_kernel(lengths_ref, recv_ref, att_ref, glob_ref, qt_ref, k_ref, vt_ref, g_ref, acc_ref):
     valid = lengths_ref[lax.axis_index("seq") // 8] // 8
-    prow = iota((HEAD_DIM, 512), 1)
     same = (iota((128, 128), 0) // HEAD_DIM == iota((128, 128), 1) // HEAD_DIM).astype(BF16)
 
     def tile_of(index):
@@ -278,39 +286,61 @@
 
     for t in range(2):
         q_t = tile_of(t).astype(F32).T.astype(BF16)
-        v_t = tile_of(4 + t).astype(F32).T
-        k = tile_of(2 + t).astype(F32)
-        k_top = jnp.maximum(k_top, jnp.max(dot_rows((k * k).astype(BF16), same)))
         for j in range(4):
-            i = t * 4 + j
             band = slice(j * HEAD_DIM, (j + 1) * HEAD_DIM)
-            live = prow * 8 + i < valid
-            vi = jnp.where(live, v_t[band], 0.0)
-            tail = jnp.where(tail_row & live[: VROWS - HEAD_DIM], 1.0, 0.0)
-            vi = jnp.concatenate([vi, tail], axis=0).astype(BF16)
-            ki = (pltpu.roll(k, 128 - j * HEAD_DIM, 1) if j else k).astype(BF16)
             for n in range(TILES):
-                at = n * QT + i * PR
-                part = slice(n * PR, (n + 1) * PR)
-                qt_ref[:, at : at + PR] = q_t[band, part]
-                vt_ref[n, :, i * PR : (i + 1) * PR] = vi[:, part]
-                k_ref[at : at + PR, :] = ki[part]
+                at = n * QT + (t * 4 + j) * PR
+                qt_ref[:, at : at + PR] = q_t[band, n * PR : (n + 1) * PR]
+
+    def finish():
+        acc = acc_ref[...]
+        o = acc[:HEAD_DIM] / acc[HEAD_DIM : HEAD_DIM + 1]
+        glob_ref[...] = o[:, COUNT:].T.astype(BF16)
+        for t in range(2):
+            bands = []
+            for j in range(4):
+                at = (t * 4 + j) * PR
+                bands.append(
+                    jnp.concatenate(
+                        [o[:, n * QT + at : n * QT + at + PR] for n in range(TILES)], axis=1
+                    )
+                )
+            packed = jnp.concatenate(bands, axis=0).T.astype(BF16)
+            att_ref[:, :, t * 128 : (t + 1) * 128] = packed.reshape(DEVICES, 2, 128)
+
+    acc_ref[...] = dot_rows(gvt, jnp.exp2(dot_rows(gk, qt_ref[...])).astype(BF16))
+    causal = place(iota((QT, QT), 1)) >= place(iota((QT, QT), 0))
+    v_t = [tile_of(4 + t).astype(F32).T for t in range(2)]
+    k_packed = [tile_of(2 + t).astype(F32) for t in range(2)]
+    for m in range(TILES):
+        lo, hi = m * QT, (m + 1) * QT
+        part = slice(m * PR, (m + 1) * PR)
+        keys, vals = [], []
+        for t in range(2):
+            k = k_packed[t][part]
+            for j in range(4):
+                keys.append(pltpu.roll(k, 128 - j * HEAD_DIM, 1) if j else k)
+                vals.append(v_t[t][j * HEAD_DIM : (j + 1) * HEAD_DIM, part])
+        k = jnp.concatenate(keys, axis=0).astype(BF16)
+        live = place(iota((HEAD_DIM, QT), 1)) + lo < valid
+        v = jnp.where(live, jnp.concatenate(vals, axis=1), 0.0)
+        tail = jnp.where(tail_row & live[: VROWS - HEAD_DIM], 1.0, 0.0)
+        v = jnp.concatenate([v, tail], axis=0).astype(BF16)
+        k_ref[lo:hi, :] = k
+        vt_ref[m] = v
+        k = k[:, :HEAD_DIM]
+        p = jnp.where(causal, jnp.exp2(dot_rows(k, qt_ref[:, lo:hi])), 0.0)
+        acc_ref[:, lo:hi] += dot_rows(v, p.astype(BF16))
+        p = jnp.exp2(dot_rows(k, qt_ref[:, hi:]))
+        acc_ref[:, hi:] += dot_rows(v, p.astype(BF16))
+    finish()
 
     q_all = qt_ref[...].astype(F32)
     q_top = jnp.max(jnp.sum(q_all * q_all, axis=0, keepdims=True))
+    for t in range(2):
+        k = k_packed[t]
+        k_top = jnp.maximum(k_top, jnp.max(dot_rows((k * k).astype(BF16), same)))
     safe = q_top * k_top * 1.05 < SAFE * SAFE
-
-    @pl.when(safe)
-    def _():
-        acc_ref[...] = dot_rows(gvt, jnp.exp2(dot_rows(gk, qt_ref[...])).astype(BF16))
-        causal = place(iota((QT, QT), 1)) >= place(iota((QT, QT), 0))
-        for m in range(TILES):
-            lo, hi = m * QT, (m + 1) * QT
-            k = k_ref[lo:hi, :HEAD_DIM]
-            p = jnp.where(causal, jnp.exp2(dot_rows(k, qt_ref[:, lo:hi])), 0.0)
-            acc_ref[:, lo:hi] += dot_rows(vt_ref[m], p.astype(BF16))
-            p = jnp.exp2(dot_rows(k, qt_ref[:, hi:]))
-            acc_ref[:, hi:] += dot_rows(vt_ref[m], p.astype(BF16))
 
     @pl.when(jnp.logical_not(safe))
     def _():
@@ -332,19 +362,7 @@
             return new
 
         lax.fori_loop(0, TILES, body, top)
-
-    acc = acc_ref[...]
-    o = acc[:HEAD_DIM] / acc[HEAD_DIM : HEAD_DIM + 1]
-    glob_ref[...] = o[:, COUNT:].T.astype(BF16)
-    for t in range(2):
-        bands = []
-        for j in range(4):
-            at = (t * 4 + j) * PR
-            bands.append(
-                jnp.concatenate([o[:, n * QT + at : n * QT + at + PR] for n in range(TILES)], axis=1)
-            )
-        packed = jnp.concatenate(bands, axis=0).T.astype(BF16)
-        att_ref[:, :, t * 128 : (t + 1) * 128] = packed.reshape(DEVICES, 2, 128)
+        finish()
 
 
 def attend_call(lengths, recv):

time: 108 us -> 116 us (1.074)
  Pallas kernels: 41.7 us -> 49.7 us
    pallas_call x1, Pallas kernels: 29.4 us -> 37.8 us  [attend_call(): pl.pallas_call(attend_kernel, in_specs=[pl.BlockSpec(memory_space=pltpu.S...]
where the time goes in v5:
time: 116 us
  Pallas kernels  49.7 us (43%)
  blocking collectives  44.3 us (38%)
  waiting for transfers between devices  14.4 us (12%)
  starting transfers between devices  6.23 us (5%)
    all_to_all x1, blocking collectives, per_device(): lax.all_to_all(payload.reshape(DEVICES, 2, 896), ('seq', 'head'), split_a...  44.3 us
    pallas_call x1, Pallas kernels, attend_call(): pl.pallas_call(attend_kernel, in_specs=[pl.BlockSpec(memory_space=pltpu.S...  37.8 us
    all_to_all x1, waiting for transfers between devices, per_device(): lax.all_to_all(att, ('seq', 'head'), split_axis=0, concat_axis=0, tiled=T...  14.4 us
    pallas_call x1, Pallas kernels, inner_call(): pl.pallas_call(inner_kernel, in_specs=[hbm] * 7, out_specs=[vmem, vmem],...  10.2 us
    all_to_all x1, starting transfers between devices, per_device(): lax.all_to_all(att, ('seq', 'head'), split_axis=0, concat_axis=0, tiled=T...  6.23 us
  transfers between devices with their start and end apart: 1, of which 1 were waited for; matrix products, arithmetic and copies ran while one was open for 1% of the time, Pallas kernels for 0%

profile of v5, /device:TPU:1, one launch (start us, length us, event | category | flops | bytes accessed | tf_op | source)
XLA Modules:
  0.0 116.1 jit_solution(6700930063672268347)
XLA Ops:
  0.6 10.2 %inner.1 = (bf16[256,512]{1,0:T(8,128)(2,1)}, bf16[16,16,2,896]{3,2,1,0:T(2,128)(2,1)}) custom-call(bf16[16,128,512]{2,1,0:T(8,128)(2,1)} %events_hbm.1, bf16[16,512]{1,0:T(8,128)(2,1)} %bitcast.9, bf16[512,1536]{1,0:T(8,128)(2,1)} %inner_qkv_hbm.1, bf16[512,512]{1,0:T(8,128)(2,1)} %inner_out_hbm.1, f32[1,512]{1,0:T(1,128)} %bitcast.10, f32[1,512]{1,0:T(1,128)} %bitcast.11, ...), custom_call_target="tpu_custom_call" | custom-call | tf_op jit(solution)/shard_map/inner/pallas_call | solution.py:232
  10.8 0.0 copy-start.2
  10.9 0.0 copy-start
  10.9 0.0 copy-start.1
  10.9 44.3 %all_to_all.10.recv_ref = bf16[256,2,896]{2,1,0:T(2,128)(2,1)S(1)} all-to-all(bf16[256,2,896]{2,1,0:T(2,128)(2,1)} %bitcast.7), channel_id=1, replica_groups=mesh['seq'=128,'head'=2] {'seq','head'}, dimensions={0} | all-to-all | bytes 1835008 | tf_op jit(solution)/shard_map/all_to_all | solution.py:449
  55.2 0.0 copy-done.2
  55.2 37.8 %attend.1 = (bf16[256,2,256]{2,1,0:T(2,128)(2,1)}, bf16[128,32]{1,0:T(8,128)(2,1)S(1)}) custom-call(s32[16]{0:T(128)S(1)} %copy-done.2, bf16[256,2,896]{2,1,0:T(2,128)(2,1)S(1)} %all_to_all.10.recv_ref), custom_call_target="tpu_custom_call" | custom-call | tf_op jit(solution)/shard_map/attend/pallas_call | solution.py:370
  93.0 6.2 %all-to-all-start.1 = ((bf16[256,2,256]{2,1,0:T(2,128)(2,1)}), bf16[256,2,256]{2,1,0:T(2,128)(2,1)S(1)}, u32[]{:S(2)}, u32[]{:S(2)}) async-start(bf16[256,2,256]{2,1,0:T(2,128)(2,1)} %get-tuple-element.7), calls=%async_computation.1 | async-start | bytes 524288 | tf_op jit(solution)/shard_map/all_to_all | solution.py:453
  99.2 0.7 reshape.31
  99.9 14.4 %all-to-all-done.1 = bf16[256,2,256]{2,1,0:T(2,128)(2,1)S(1)} async-done(((bf16[256,2,256]{2,1,0:T(2,128)(2,1)}), bf16[256,2,256]{2,1,0:T(2,128)(2,1)S(1)}, u32[]{:S(2)}, u32[]{:S(2)}) %all-to-all-start.1) | async-done | bytes 262176 | tf_op jit(solution)/shard_map/all_to_all | solution.py:453
  114.3 0.0 copy-done
  114.4 0.0 copy-done.1
  114.4 1.7 %output.1 = bf16[256,512]{1,0:T(8,128)(2,1)} custom-call(bf16[16,16,2,256]{3,2,1,0:T(2,128)(2,1)S(1)} %bitcast.6, bf16[256,512]{1,0:T(8,128)(2,1)S(1)} %copy-done.1, bf16[512,512]{1,0:T(8,128)(2,1)S(1)} %copy-done), custom_call_target="tpu_custom_call" | custom-call | tf_op jit(solution)/shard_map/output/pallas_call | solution.py:415
Async XLA Ops:
  10.8 44.3 %copy-start.2 = (s32[16]{0:T(128)S(1)}, s32[16]{0:T(128)}, u32[]{:S(2)}) copy-start(s32[16]{0:T(128)} %lengths_ref.1) | copy-start | bytes 196
  10.9 103.5 %copy-start = (bf16[512,512]{1,0:T(8,128)(2,1)S(1)}, bf16[512,512]{1,0:T(8,128)(2,1)}, u32[]{:S(2)}) copy-start(bf16[512,512]{1,0:T(8,128)(2,1)} %mixed_out_ref.1) | copy-start | bytes 1572868
  10.9 103.5 %copy-start.1 = (bf16[256,512]{1,0:T(8,128)(2,1)S(1)}, bf16[256,512]{1,0:T(8,128)(2,1)}, u32[]{:S(2)}) copy-start(bf16[256,512]{1,0:T(8,128)(2,1)} %get-tuple-element.8.merged_ref) | copy-start | bytes 786436
  93.0 21.4 %all-to-all-start.1 = ((bf16[256,2,256]{2,1,0:T(2,128)(2,1)}), bf16[256,2,256]{2,1,0:T(2,128)(2,1)S(1)}, u32[]{:S(2)}, u32[]{:S(2)}) async-start(bf16[256,2,256]{2,1,0:T(2,128)(2,1)} %get-tuple-element.7), calls=%async_computation.1 | async-start | bytes 524288 | tf_op jit(solution)/shard_map/all_to_all | solution.py:453

commit v6 on v5

--- a/solution.py
+++ b/solution.py
@@ -51,6 +51,8 @@
     merge_gain_hbm,
     global_gain_hbm,
     mixed_qkv_hbm,
+    merged_hbm,
+    payload_hbm,
     merged_ref,
     payload_ref,
     normed_ref,
@@ -90,12 +92,14 @@
 
     def project(step):
         if step == 0:
-            for copy in copies[:4]:
+            copies[0].wait()
+        x = events_ref[step * STEP_USERS : (step + 1) * STEP_USERS]
+        x = x.reshape(STEP_USERS * SPAN, WIDTH)
+        if step == 0:
+            for copy in copies[1:4]:
                 copy.wait()
             for copy in copies[4:]:
                 copy.start()
-        x = events_ref[step * STEP_USERS : (step + 1) * STEP_USERS]
-        x = x.reshape(STEP_USERS * SPAN, WIDTH)
         return x, dot_rows(x, inner_qkv_ref[...]).astype(BF16)
 
     def score(qkv):
@@ -158,8 +162,61 @@
         for c in range(4):
             normed_ref[c, step * rows : (step + 1) * rows, :] = normed[:, c * 128 : (c + 1) * 128]
 
-    held, scores, spreads = {}, {}, {}
-    for turn in range(STEPS + 3):
+    half = 2 * STEP_USERS
+    lane_block = iota((half, 128), 1) // HEAD_DIM
+
+    def pack(step):
+        users = slice(step * STEP_USERS, (step + 1) * STEP_USERS)
+        first = step * STEP_USERS * TOKENS
+        slab_rows = jnp.concatenate(
+            [
+                jnp.concatenate(
+                    [normed_ref[c, pl.ds(first + i, half, stride=8), :] for i in range(8)], axis=0
+                ).astype(BF16)
+                for c in range(4)
+            ],
+            axis=1,
+        )
+        for c in range(3):
+            for hp in range(2):
+                col = c * 512 + hp * 256
+                pair = dot_rows(slab_rows, mixed_qkv_ref[:, col : col + 256])
+                if c == 0:
+                    pair = pair * SCORE_SCALE
+                for ht in (2 * hp, 2 * hp + 1):
+                    part = pair[:, (ht % 2) * 128 : (ht % 2 + 1) * 128]
+                    for t in range(2):
+                        base = [part[(t * 4 + j) * half : (t * 4 + j + 1) * half] for j in range(4)]
+                        for hh in range(4):
+                            out = None
+                            for j in range(4):
+                                shift = (HEAD_DIM * (j - hh)) % 128
+                                moved = pltpu.roll(base[j], shift, 1) if shift else base[j]
+                                out = moved if j == 0 else jnp.where(lane_block == j, moved, out)
+                            tile = (c * 2 + t) * 128
+                            payload_ref[users, ht * 4 + hh, :, tile : tile + 128] = out.astype(
+                                BF16
+                            ).reshape(STEP_USERS, 2, 128)
+
+    def pack_globals():
+        gnormed = norm_f32(tokens_ref[...].astype(F32), global_gain_ref[...]).astype(BF16)
+        block16 = iota((USERS, 128), 1) // HEAD_DIM
+        gqkv = [dot_rows(gnormed, mixed_qkv_ref[:, c * 512 : (c + 1) * 512]) for c in range(3)]
+        gqkv[0] = gqkv[0] * SCORE_SCALE
+        for ht in range(4):
+            sect = [part[:, ht * 128 : (ht + 1) * 128] for part in gqkv]
+            for hh in range(4):
+                out = jnp.zeros((USERS, 128), F32)
+                for c in range(3):
+                    shift = (HEAD_DIM * (c - hh)) % 128
+                    moved = pltpu.roll(sect[c], shift, 1) if shift else sect[c]
+                    out = jnp.where(block16 == c, moved, out)
+                payload_ref[:, ht * 4 + hh, :, 768:896] = jnp.broadcast_to(
+                    out[:, None, :], (USERS, 2, 128)
+                ).astype(BF16)
+
+    held, scores, spreads, sent = {}, {}, {}, []
+    for turn in range(STEPS + 4):
         if turn < STEPS:
             held[turn] = project(turn)
         if 0 <= turn - 1 < STEPS:
@@ -168,76 +225,40 @@
             spreads[turn - 2] = pool_weights(scores[turn - 2])
         if 0 <= turn - 3 < STEPS:
             merge(turn - 3, *held[turn - 3], spreads[turn - 3])
+        if 0 <= turn - 4 < STEPS:
+            pack(turn - 4)
+            users = slice((turn - 4) * STEP_USERS, (turn - 3) * STEP_USERS)
+            sent.append(
+                pltpu.make_async_copy(
+                    payload_ref.at[users], payload_hbm.at[users], sems.at[STEPS + 10 + turn - 4]
+                )
+            )
+            sent[-1].start()
         if turn == 0:
-            for copy in copies[4 : 5 + STEPS]:
+            for copy in copies[4:]:
                 copy.wait()
-
-    for copy in copies[5 + STEPS :]:
+        if turn == 1:
+            pack_globals()
+        if turn == STEPS + 2:
+            sent.append(pltpu.make_async_copy(merged_ref, merged_hbm, sems.at[2 * STEPS + 10]))
+            sent[-1].start()
+    for copy in sent:
         copy.wait()
-    slab_rows = jnp.concatenate(
-        [
-            jnp.concatenate(
-                [normed_ref[c, pl.ds(i, 2 * USERS, stride=8), :] for i in range(8)], axis=0
-            ).astype(BF16)
-            for c in range(4)
-        ],
-        axis=1,
-    )
-    lane_block = iota((2 * USERS, 128), 1) // HEAD_DIM
-    for c in range(3):
-        for hp in range(2):
-            col = c * 512 + hp * 256
-            pair = dot_rows(slab_rows, mixed_qkv_ref[:, col : col + 256])
-            if c == 0:
-                pair = pair * SCORE_SCALE
-            for ht in (2 * hp, 2 * hp + 1):
-                part = pair[:, (ht % 2) * 128 : (ht % 2 + 1) * 128]
-                for t in range(2):
-                    base = [
-                        part[(t * 4 + j) * 2 * USERS : (t * 4 + j + 1) * 2 * USERS]
-                        for j in range(4)
-                    ]
-                    for hh in range(4):
-                        out = None
-                        for j in range(4):
-                            shift = (HEAD_DIM * (j - hh)) % 128
-                            moved = pltpu.roll(base[j], shift, 1) if shift else base[j]
-                            out = moved if j == 0 else jnp.where(lane_block == j, moved, out)
-                        tile = (c * 2 + t) * 128
-                        payload_ref[:, ht * 4 + hh, :, tile : tile + 128] = out.astype(
-                            BF16
-                        ).reshape(USERS, 2, 128)
-    gnormed = norm_f32(tokens_ref[...].astype(F32), global_gain_ref[...]).astype(BF16)
-    block16 = iota((USERS, 128), 1) // HEAD_DIM
-    gqkv = [
-        dot_rows(gnormed, mixed_qkv_ref[:, c * 512 : (c + 1) * 512]) for c in range(3)
-    ]
-    gqkv[0] = gqkv[0] * SCORE_SCALE
-    for ht in range(4):
-        sect = [part[:, ht * 128 : (ht + 1) * 128] for part in gqkv]
-        for hh in range(4):
-            out = jnp.zeros((USERS, 128), F32)
-            for c in range(3):
-                shift = (HEAD_DIM * (c - hh)) % 128
-                moved = pltpu.roll(sect[c], shift, 1) if shift else sect[c]
-                out = jnp.where(block16 == c, moved, out)
-            payload_ref[:, ht * 4 + hh, :, 768:896] = jnp.broadcast_to(
-                out[:, None, :], (USERS, 2, 128)
-            ).astype(BF16)
 
 
 def inner_call(events, tokens, inner_qkv, inner_out, merge_gain, global_gain, mixed_qkv):
     hbm = pl.BlockSpec(memory_space=pl.ANY)
-    vmem = pl.BlockSpec(memory_space=pltpu.VMEM)
     return pl.pallas_call(
         inner_kernel,
         in_specs=[hbm] * 7,
-        out_specs=[vmem, vmem],
+        out_specs=[hbm, hbm],
         out_shape=[
             jax.ShapeDtypeStruct((USERS * TOKENS, WIDTH), BF16),
             jax.ShapeDtypeStruct((USERS, HEADS, 2, 896), BF16),
         ],
         scratch_shapes=[
+            pltpu.VMEM((USERS * TOKENS, WIDTH), BF16),
+            pltpu.VMEM((USERS, HEADS, 2, 896), BF16),
             pltpu.VMEM((4, USERS * TOKENS, 128), F32),
             pltpu.VMEM((USERS, SPAN, WIDTH), BF16),
             pltpu.VMEM((USERS, WIDTH), BF16),
@@ -246,7 +267,7 @@
             pltpu.VMEM((1, WIDTH), F32),
             pltpu.VMEM((1, WIDTH), F32),
             pltpu.VMEM((WIDTH, 3 * WIDTH), BF16),
-            pltpu.SemaphoreType.DMA((STEPS + 10,)),
+            pltpu.SemaphoreType.DMA((2 * STEPS + 11,)),
         ],
         compiler_params=pltpu.CompilerParams(vmem_limit_bytes=60 * 2**20),
         name="inner",
@@ -329,10 +350,9 @@
         k_ref[lo:hi, :] = k
         vt_ref[m] = v
         k = k[:, :HEAD_DIM]
-        p = jnp.where(causal, jnp.exp2(dot_rows(k, qt_ref[:, lo:hi])), 0.0)
-        acc_ref[:, lo:hi] += dot_rows(v, p.astype(BF16))
-        p = jnp.exp2(dot_rows(k, qt_ref[:, hi:]))
-        acc_ref[:, hi:] += dot_rows(v, p.astype(BF16))
+        p = jnp.exp2(dot_rows(k, qt_ref[:, lo:]))
+        p = jnp.concatenate([jnp.where(causal, p[:, :QT], 0.0), p[:, QT:]], axis=1)
+        acc_ref[:, lo:] += dot_rows(v, p.astype(BF16))
     finish()
 
     q_all = qt_ref[...].astype(F32)

time: 116 us -> 115 us (level)
  no operation moved by 1% of the time
where the time goes in v6:
time: 115 us
  Pallas kernels  49 us (43%)
  blocking collectives  44.3 us (39%)
  waiting for transfers between devices  14.4 us (13%)
  starting transfers between devices  6.23 us (5%)
    all_to_all x1, blocking collectives, per_device(): lax.all_to_all(payload.reshape(DEVICES, 2, 896), ('seq', 'head'), split_a...  44.3 us
    pallas_call x1, Pallas kernels, attend_call(): pl.pallas_call(attend_kernel, in_specs=[pl.BlockSpec(memory_space=pltpu.S...  37.4 us
    all_to_all x1, waiting for transfers between devices, per_device(): lax.all_to_all(att, ('seq', 'head'), split_axis=0, concat_axis=0, tiled=T...  14.4 us
    pallas_call x1, Pallas kernels, inner_call(): pl.pallas_call(inner_kernel, in_specs=[hbm] * 7, out_specs=[hbm, hbm], ou...  9.89 us
    all_to_all x1, starting transfers between devices, per_device(): lax.all_to_all(att, ('seq', 'head'), split_axis=0, concat_axis=0, tiled=T...  6.23 us
  transfers between devices with their start and end apart: 1, of which 1 were waited for; matrix products, arithmetic and copies ran while one was open for 1% of the time, Pallas kernels for 0%

profile of v6, /device:TPU:1, one launch (start us, length us, event | category | flops | bytes accessed | tf_op | source)
XLA Modules:
  0.0 115.3 jit_solution(1228588820670910156)
XLA Ops:
  0.6 9.9 %inner.1 = (bf16[256,512]{1,0:T(8,128)(2,1)}, bf16[16,16,2,896]{3,2,1,0:T(2,128)(2,1)}) custom-call(bf16[16,128,512]{2,1,0:T(8,128)(2,1)} %events_hbm.1, bf16[16,512]{1,0:T(8,128)(2,1)} %bitcast.9, bf16[512,1536]{1,0:T(8,128)(2,1)} %inner_qkv_hbm.1, bf16[512,512]{1,0:T(8,128)(2,1)} %inner_out_hbm.1, f32[1,512]{1,0:T(1,128)} %bitcast.10, f32[1,512]{1,0:T(1,128)} %bitcast.11, ...), custom_call_target="tpu_custom_call" | custom-call | tf_op jit(solution)/shard_map/inner/pallas_call | solution.py:251
  10.5 0.0 copy-start.2
  10.5 0.0 copy-start
  10.6 0.0 copy-start.1
  10.6 44.3 %all_to_all.10.recv_ref = bf16[256,2,896]{2,1,0:T(2,128)(2,1)S(1)} all-to-all(bf16[256,2,896]{2,1,0:T(2,128)(2,1)} %bitcast.7), channel_id=1, replica_groups=mesh['seq'=128,'head'=2] {'seq','head'}, dimensions={0} | all-to-all | bytes 1835008 | tf_op jit(solution)/shard_map/all_to_all | solution.py:469
  54.8 0.0 copy-done.2
  54.9 37.4 %attend.1 = (bf16[256,2,256]{2,1,0:T(2,128)(2,1)}, bf16[128,32]{1,0:T(8,128)(2,1)S(1)}) custom-call(s32[16]{0:T(128)S(1)} %copy-done.2, bf16[256,2,896]{2,1,0:T(2,128)(2,1)S(1)} %all_to_all.10.recv_ref), custom_call_target="tpu_custom_call" | custom-call | tf_op jit(solution)/shard_map/attend/pallas_call | solution.py:390
  92.2 6.2 %all-to-all-start.1 = ((bf16[256,2,256]{2,1,0:T(2,128)(2,1)}), bf16[256,2,256]{2,1,0:T(2,128)(2,1)S(1)}, u32[]{:S(2)}, u32[]{:S(2)}) async-start(bf16[256,2,256]{2,1,0:T(2,128)(2,1)} %get-tuple-element.7), calls=%async_computation.1 | async-start | bytes 524288 | tf_op jit(solution)/shard_map/all_to_all | solution.py:473
  98.5 0.7 reshape.31
  99.2 14.4 %all-to-all-done.1 = bf16[256,2,256]{2,1,0:T(2,128)(2,1)S(1)} async-done(((bf16[256,2,256]{2,1,0:T(2,128)(2,1)}), bf16[256,2,256]{2,1,0:T(2,128)(2,1)S(1)}, u32[]{:S(2)}, u32[]{:S(2)}) %all-to-all-start.1) | async-done | bytes 262176 | tf_op jit(solution)/shard_map/all_to_all | solution.py:473
  113.6 0.0 copy-done
  113.6 0.0 copy-done.1
  113.6 1.7 %output.1 = bf16[256,512]{1,0:T(8,128)(2,1)} custom-call(bf16[16,16,2,256]{3,2,1,0:T(2,128)(2,1)S(1)} %bitcast.6, bf16[256,512]{1,0:T(8,128)(2,1)S(1)} %copy-done.1, bf16[512,512]{1,0:T(8,128)(2,1)S(1)} %copy-done), custom_call_target="tpu_custom_call" | custom-call | tf_op jit(solution)/shard_map/output/pallas_call | solution.py:435
Async XLA Ops:
  10.5 44.3 %copy-start.2 = (s32[16]{0:T(128)S(1)}, s32[16]{0:T(128)}, u32[]{:S(2)}) copy-start(s32[16]{0:T(128)} %lengths_ref.1) | copy-start | bytes 196
  10.5 103.0 %copy-start = (bf16[512,512]{1,0:T(8,128)(2,1)S(1)}, bf16[512,512]{1,0:T(8,128)(2,1)}, u32[]{:S(2)}) copy-start(bf16[512,512]{1,0:T(8,128)(2,1)} %mixed_out_ref.1) | copy-start | bytes 1572868
  10.6 103.0 %copy-start.1 = (bf16[256,512]{1,0:T(8,128)(2,1)S(1)}, bf16[256,512]{1,0:T(8,128)(2,1)}, u32[]{:S(2)}) copy-start(bf16[256,512]{1,0:T(8,128)(2,1)} %get-tuple-element.8.merged_ref) | copy-start | bytes 786436
  92.2 21.4 %all-to-all-start.1 = ((bf16[256,2,256]{2,1,0:T(2,128)(2,1)}), bf16[256,2,256]{2,1,0:T(2,128)(2,1)S(1)}, u32[]{:S(2)}, u32[]{:S(2)}) async-start(bf16[256,2,256]{2,1,0:T(2,128)(2,1)} %get-tuple-element.7), calls=%async_computation.1 | async-start | bytes 524288 | tf_op jit(solution)/shard_map/all_to_all | solution.py:473

commit v7 on v6

--- a/solution.py
+++ b/solution.py
@@ -24,6 +24,7 @@
 SCORE_SCALE = math.log2(math.e) / math.sqrt(HEAD_DIM)
 SAFE = 100.0
 LOW = -1e30
+PAD = 8
 
 
 def dot_rows(a, b):
@@ -259,7 +260,7 @@
         scratch_shapes=[
             pltpu.VMEM((USERS * TOKENS, WIDTH), BF16),
             pltpu.VMEM((USERS, HEADS, 2, 896), BF16),
-            pltpu.VMEM((4, USERS * TOKENS, 128), F32),
+            pltpu.VMEM((4, USERS * TOKENS + PAD, 128), F32),
             pltpu.VMEM((USERS, SPAN, WIDTH), BF16),
             pltpu.VMEM((USERS, WIDTH), BF16),
             pltpu.VMEM((WIDTH, 3 * WIDTH), BF16),
@@ -292,7 +293,7 @@
     def tile_of(index):
         return recv_ref[:, :, index * 128 : (index + 1) * 128].reshape(512, 128)
 
-    g_ref[...] = tile_of(6).astype(F32)
+    g_ref[0:512, :] = tile_of(6).astype(F32)
     g = g_ref[pl.ds(0, GLOBALS, stride=4), :]
     gt = g.T
     gk = pltpu.roll(g, 128 - HEAD_DIM, 1).astype(BF16)[:, :HEAD_DIM]
@@ -399,7 +400,7 @@
             pltpu.VMEM((HEAD_DIM, QUERIES), BF16),
             pltpu.VMEM((COUNT, 128), BF16),
             pltpu.VMEM((TILES, VROWS, QT), BF16),
-            pltpu.VMEM((512, 128), F32),
+            pltpu.VMEM((512 + PAD, 128), F32),
             pltpu.VMEM((VROWS, QUERIES), F32),
         ],
         compiler_params=pltpu.CompilerParams(vmem_limit_bytes=32 * 2**20),
@@ -427,7 +428,7 @@
         for i in range(8):
             rows = slice(i * 2 * USERS, (i + 1) * 2 * USERS)
             sum_ref[c, pl.ds(i, 2 * USERS, stride=8), :] = prod[rows, cols]
-        out_ref[:, cols] = (merged_ref[:, cols].astype(F32) + sum_ref[c]).astype(BF16)
+        out_ref[:, cols] = (merged_ref[:, cols].astype(F32) + sum_ref[c, : USERS * TOKENS]).astype(BF16)
 
 
 def output_call(back, merged, mixed_out):
@@ -439,7 +440,7 @@
         out_shape=jax.ShapeDtypeStruct((USERS * TOKENS, WIDTH), BF16),
         scratch_shapes=[
             pltpu.VMEM((HEADS * 128, WIDTH), BF16),
-            pltpu.VMEM((4, USERS * TOKENS, 128), F32),
+            pltpu.VMEM((4, USERS * TOKENS + PAD, 128), F32),
         ],
         compiler_params=pltpu.CompilerParams(vmem_limit_bytes=16 * 2**20),
         name="output",

time: 115 us -> 116 us (level)
  no operation moved by 1% of the time
where the time goes in v7:
time: 116 us; the launch traced here: 115 us
  Pallas kernels  49 us (42%)
  blocking collectives  44.3 us (38%)
  waiting for transfers between devices  14.4 us (12%)
  starting transfers between devices  6.24 us (5%)
    all_to_all x1, blocking collectives, per_device(): lax.all_to_all(payload.reshape(DEVICES, 2, 896), ('seq', 'head'), split_a...  44.3 us
    pallas_call x1, Pallas kernels, attend_call(): pl.pallas_call(attend_kernel, in_specs=[pl.BlockSpec(memory_space=pltpu.S...  37.4 us
    all_to_all x1, waiting for transfers between devices, per_device(): lax.all_to_all(att, ('seq', 'head'), split_axis=0, concat_axis=0, tiled=T...  14.4 us
    pallas_call x1, Pallas kernels, inner_call(): pl.pallas_call(inner_kernel, in_specs=[hbm] * 7, out_specs=[hbm, hbm], ou...  9.89 us
    all_to_all x1, starting transfers between devices, per_device(): lax.all_to_all(att, ('seq', 'head'), split_axis=0, concat_axis=0, tiled=T...  6.24 us
  transfers between devices with their start and end apart: 1, of which 1 were waited for; matrix products, arithmetic and copies ran while one was open for 1% of the time, Pallas kernels for 0%

profile of v7, /device:TPU:1, one launch (start us, length us, event | category | flops | bytes accessed | tf_op | source)
XLA Modules:
  0.0 115.3 jit_solution(16027532792891340979)
XLA Ops:
  0.6 9.9 %inner.1 = (bf16[256,512]{1,0:T(8,128)(2,1)}, bf16[16,16,2,896]{3,2,1,0:T(2,128)(2,1)}) custom-call(bf16[16,128,512]{2,1,0:T(8,128)(2,1)} %events_hbm.1, bf16[16,512]{1,0:T(8,128)(2,1)} %bitcast.9, bf16[512,1536]{1,0:T(8,128)(2,1)} %inner_qkv_hbm.1, bf16[512,512]{1,0:T(8,128)(2,1)} %inner_out_hbm.1, f32[1,512]{1,0:T(1,128)} %bitcast.10, f32[1,512]{1,0:T(1,128)} %bitcast.11, ...), custom_call_target="tpu_custom_call" | custom-call | tf_op jit(solution)/shard_map/inner/pallas_call | solution.py:252
  10.5 0.0 copy-start.2
  10.5 0.0 copy-start
  10.6 0.0 copy-start.1
  10.6 44.3 %all_to_all.10.recv_ref = bf16[256,2,896]{2,1,0:T(2,128)(2,1)S(1)} all-to-all(bf16[256,2,896]{2,1,0:T(2,128)(2,1)} %bitcast.7), channel_id=1, replica_groups=mesh['seq'=128,'head'=2] {'seq','head'}, dimensions={0} | all-to-all | bytes 1835008 | tf_op jit(solution)/shard_map/all_to_all | solution.py:470
  54.8 0.0 copy-done.2
  54.8 37.4 %attend.1 = (bf16[256,2,256]{2,1,0:T(2,128)(2,1)}, bf16[128,32]{1,0:T(8,128)(2,1)S(1)}) custom-call(s32[16]{0:T(128)S(1)} %copy-done.2, bf16[256,2,896]{2,1,0:T(2,128)(2,1)S(1)} %all_to_all.10.recv_ref), custom_call_target="tpu_custom_call" | custom-call | tf_op jit(solution)/shard_map/attend/pallas_call | solution.py:391
  92.2 6.2 %all-to-all-start.1 = ((bf16[256,2,256]{2,1,0:T(2,128)(2,1)}), bf16[256,2,256]{2,1,0:T(2,128)(2,1)S(1)}, u32[]{:S(2)}, u32[]{:S(2)}) async-start(bf16[256,2,256]{2,1,0:T(2,128)(2,1)} %get-tuple-element.7), calls=%async_computation.1 | async-start | bytes 524288 | tf_op jit(solution)/shard_map/all_to_all | solution.py:474
  98.5 0.7 reshape.31
  99.2 14.4 %all-to-all-done.1 = bf16[256,2,256]{2,1,0:T(2,128)(2,1)S(1)} async-done(((bf16[256,2,256]{2,1,0:T(2,128)(2,1)}), bf16[256,2,256]{2,1,0:T(2,128)(2,1)S(1)}, u32[]{:S(2)}, u32[]{:S(2)}) %all-to-all-start.1) | async-done | bytes 262176 | tf_op jit(solution)/shard_map/all_to_all | solution.py:474
  113.6 0.0 copy-done
  113.6 0.0 copy-done.1
  113.6 1.7 %output.1 = bf16[256,512]{1,0:T(8,128)(2,1)} custom-call(bf16[16,16,2,256]{3,2,1,0:T(2,128)(2,1)S(1)} %bitcast.6, bf16[256,512]{1,0:T(8,128)(2,1)S(1)} %copy-done.1, bf16[512,512]{1,0:T(8,128)(2,1)S(1)} %copy-done), custom_call_target="tpu_custom_call" | custom-call | tf_op jit(solution)/shard_map/output/pallas_call | solution.py:436
Async XLA Ops:
  10.5 44.3 %copy-start.2 = (s32[16]{0:T(128)S(1)}, s32[16]{0:T(128)}, u32[]{:S(2)}) copy-start(s32[16]{0:T(128)} %lengths_ref.1) | copy-start | bytes 196
  10.5 103.1 %copy-start = (bf16[512,512]{1,0:T(8,128)(2,1)S(1)}, bf16[512,512]{1,0:T(8,128)(2,1)}, u32[]{:S(2)}) copy-start(bf16[512,512]{1,0:T(8,128)(2,1)} %mixed_out_ref.1) | copy-start | bytes 1572868
  10.6 103.1 %copy-start.1 = (bf16[256,512]{1,0:T(8,128)(2,1)S(1)}, bf16[256,512]{1,0:T(8,128)(2,1)}, u32[]{:S(2)}) copy-start(bf16[256,512]{1,0:T(8,128)(2,1)} %get-tuple-element.8.merged_ref) | copy-start | bytes 786436
  92.2 21.4 %all-to-all-start.1 = ((bf16[256,2,256]{2,1,0:T(2,128)(2,1)}), bf16[256,2,256]{2,1,0:T(2,128)(2,1)S(1)}, u32[]{:S(2)}, u32[]{:S(2)}) async-start(bf16[256,2,256]{2,1,0:T(2,128)(2,1)} %get-tuple-element.7), calls=%async_computation.1 | async-start | bytes 524288 | tf_op jit(solution)/shard_map/all_to_all | solution.py:474

commit v8 on v7

--- a/solution.py
+++ b/solution.py
@@ -317,7 +317,14 @@
     def finish():
         acc = acc_ref[...]
         o = acc[:HEAD_DIM] / acc[HEAD_DIM : HEAD_DIM + 1]
-        glob_ref[...] = o[:, COUNT:].T.astype(BF16)
+        g_ref[0:GLOBALS, 0:HEAD_DIM] = o[:, COUNT:].T
+        lane = iota((HEAD_DIM, 128), 1) // HEAD_DIM
+        rows = g_ref[pl.ds(0, GLOBALS // 4, stride=4), :]
+        for n in range(1, 4):
+            moved = pltpu.roll(g_ref[pl.ds(n, GLOBALS // 4, stride=4), :], n * HEAD_DIM, 1)
+            rows = jnp.where(lane == n, moved, rows)
+        for n in range(GLOBALS // 4):
+            glob_ref[0, :, n * 128 : (n + 1) * 128] = rows[n : n + 1].astype(BF16)
         for t in range(2):
             bands = []
             for j in range(4):
@@ -394,7 +401,7 @@
         out_specs=[vmem, vmem],
         out_shape=[
             jax.ShapeDtypeStruct((DEVICES, 2, 256), BF16),
-            jax.ShapeDtypeStruct((GLOBALS, HEAD_DIM), BF16),
+            jax.ShapeDtypeStruct((1, 1, GLOBALS * HEAD_DIM), BF16),
         ],
         scratch_shapes=[
             pltpu.VMEM((HEAD_DIM, QUERIES), BF16),
@@ -473,7 +480,7 @@
     att, glob = attend_call(lengths, arrived)
     back = lax.all_to_all(att, ("seq", "head"), split_axis=0, concat_axis=0, tiled=True)
     out = output_call(back.reshape(USERS, HEADS, 2, 256), merged, mixed_out)
-    return (out.reshape(USERS, TOKENS, WIDTH), glob.reshape(1, 1, GLOBALS * HEAD_DIM))
+    return (out.reshape(USERS, TOKENS, WIDTH), glob)
 
 
 def solution(mesh):

time: 116 us -> 115 us (level)
  blocking collectives: 44.3 us -> 65.4 us
  waiting for transfers between devices: 14.4 us -> 0 us
  starting transfers between devices: 6.24 us -> 0 us
    all_to_all x0 -> x1, blocking collectives: none -> 21.2 us  [per_device(): lax.all_to_all(att, ('seq', 'head'), split_axis=0, concat_axis=0, tiled=T...]
    all_to_all x1 -> x0, waiting for transfers between devices: 14.4 us -> none  [per_device(): lax.all_to_all(att, ('seq', 'head'), split_axis=0, concat_axis=0, tiled=T...]
    all_to_all x1 -> x0, starting transfers between devices: 6.24 us -> none  [per_device(): lax.all_to_all(att, ('seq', 'head'), split_axis=0, concat_axis=0, tiled=T...]
  transfers between devices with their start and end apart: 1 -> 0, of which waited for: 1 -> 0; matrix products, arithmetic and copies ran while one was open for 1% -> 0% of each run, Pallas kernels for 0% -> 0%
where the time goes in v8:
time: 115 us
  blocking collectives  65.4 us (57%)
  Pallas kernels  48.9 us (43%)
    all_to_all x1, blocking collectives, per_device(): lax.all_to_all(payload.reshape(DEVICES, 2, 896), ('seq', 'head'), split_a...  44.3 us
    pallas_call x1, Pallas kernels, attend_call(): pl.pallas_call(attend_kernel, in_specs=[pl.BlockSpec(memory_space=pltpu.S...  37.3 us
    all_to_all x1, blocking collectives, per_device(): lax.all_to_all(att, ('seq', 'head'), split_axis=0, concat_axis=0, tiled=T...  21.2 us
    pallas_call x1, Pallas kernels, inner_call(): pl.pallas_call(inner_kernel, in_specs=[hbm] * 7, out_specs=[hbm, hbm], ou...  9.88 us

profile of v8, /device:TPU:1, one launch (start us, length us, event | category | flops | bytes accessed | tf_op | source)
XLA Modules:
  0.0 115.0 jit_solution(12041951457869869153)
XLA Ops:
  0.6 9.9 %inner.1 = (bf16[256,512]{1,0:T(8,128)(2,1)}, bf16[16,16,2,896]{3,2,1,0:T(2,128)(2,1)}) custom-call(bf16[16,128,512]{2,1,0:T(8,128)(2,1)} %events_hbm.1, bf16[16,512]{1,0:T(8,128)(2,1)} %bitcast.9, bf16[512,1536]{1,0:T(8,128)(2,1)} %inner_qkv_hbm.1, bf16[512,512]{1,0:T(8,128)(2,1)} %inner_out_hbm.1, f32[1,512]{1,0:T(1,128)} %bitcast.10, f32[1,512]{1,0:T(1,128)} %bitcast.11, ...), custom_call_target="tpu_custom_call" | custom-call | tf_op jit(solution)/shard_map/inner/pallas_call | solution.py:252
  10.5 0.0 copy-start.2
  10.5 0.0 copy-start
  10.5 0.0 copy-start.1
  10.6 44.3 %all_to_all.10.recv_ref = bf16[256,2,896]{2,1,0:T(2,128)(2,1)S(1)} all-to-all(bf16[256,2,896]{2,1,0:T(2,128)(2,1)} %bitcast.7), channel_id=1, replica_groups=mesh['seq'=128,'head'=2] {'seq','head'}, dimensions={0} | all-to-all | bytes 1835008 | tf_op jit(solution)/shard_map/all_to_all | solution.py:477
  54.8 0.0 copy-done.2
  54.8 37.3 %attend.1 = (bf16[256,2,256]{2,1,0:T(2,128)(2,1)S(1)}, bf16[1,1,4096]{2,1,0:T(2,128)(2,1)}) custom-call(s32[16]{0:T(128)S(1)} %copy-done.2, bf16[256,2,896]{2,1,0:T(2,128)(2,1)S(1)} %all_to_all.10.recv_ref), custom_call_target="tpu_custom_call" | custom-call | tf_op jit(solution)/shard_map/attend/pallas_call | solution.py:398
  92.2 21.2 %all_to_all.11 = bf16[256,2,256]{2,1,0:T(2,128)(2,1)S(1)} all-to-all(bf16[256,2,256]{2,1,0:T(2,128)(2,1)S(1)} %get-tuple-element.7), channel_id=1, replica_groups=mesh['seq'=128,'head'=2] {'seq','head'}, dimensions={0} | all-to-all | bytes 524288 | tf_op jit(solution)/shard_map/all_to_all | solution.py:481
  113.3 0.0 copy-done
  113.3 0.0 copy-done.1
  113.3 1.7 %output.1 = bf16[256,512]{1,0:T(8,128)(2,1)} custom-call(bf16[16,16,2,256]{3,2,1,0:T(2,128)(2,1)S(1)} %bitcast.6, bf16[256,512]{1,0:T(8,128)(2,1)S(1)} %copy-done.1, bf16[512,512]{1,0:T(8,128)(2,1)S(1)} %copy-done), custom_call_target="tpu_custom_call" | custom-call | tf_op jit(solution)/shard_map/output/pallas_call | solution.py:443
Async XLA Ops:
  10.5 44.3 %copy-start.2 = (s32[16]{0:T(128)S(1)}, s32[16]{0:T(128)}, u32[]{:S(2)}) copy-start(s32[16]{0:T(128)} %lengths_ref.1) | copy-start | bytes 196
  10.5 102.8 %copy-start = (bf16[512,512]{1,0:T(8,128)(2,1)S(1)}, bf16[512,512]{1,0:T(8,128)(2,1)}, u32[]{:S(2)}) copy-start(bf16[512,512]{1,0:T(8,128)(2,1)} %mixed_out_ref.1) | copy-start | bytes 1572868
  10.5 102.8 %copy-start.1 = (bf16[256,512]{1,0:T(8,128)(2,1)S(1)}, bf16[256,512]{1,0:T(8,128)(2,1)}, u32[]{:S(2)}) copy-start(bf16[256,512]{1,0:T(8,128)(2,1)} %get-tuple-element.8.merged_ref) | copy-start | bytes 786436

commit v9 on v8

--- a/solution.py
+++ b/solution.py
@@ -125,9 +125,7 @@
         w = expd / jnp.sum(expd, axis=1, keepdims=True)
         w = w.reshape(STEP_USERS * 64, 128)
         same = (iota((128, 128), 0) // 8 == iota((128, 128), 1) // 8).astype(BF16)
-        w_hi = w.astype(BF16)
-        w_lo = (w - w_hi.astype(F32)).astype(BF16)
-        wm = (dot_rows(w_hi, same) + dot_rows(w_lo, same)) * 0.125
+        wm = dot_rows(w.astype(BF16), same) * 0.125
         wm = wm.reshape(STEP_USERS * 8, 8, 128)
         on_diag = iota((8, 128), 0) == iota((8, 128), 1) % 8
         row = jnp.sum(jnp.where(on_diag[None], wm, 0.0), axis=1, keepdims=True)

time: 115 us -> 115 us (level)
  no operation moved by 1% of the time
where the time goes in v9:
time: 115 us
  blocking collectives  65.4 us (57%)
  Pallas kernels  48.9 us (43%)
    all_to_all x1, blocking collectives, per_device(): lax.all_to_all(payload.reshape(DEVICES, 2, 896), ('seq', 'head'), split_a...  44.3 us
    pallas_call x1, Pallas kernels, attend_call(): pl.pallas_call(attend_kernel, in_specs=[pl.BlockSpec(memory_space=pltpu.S...  37.3 us
    all_to_all x1, blocking collectives, per_device(): lax.all_to_all(att, ('seq', 'head'), split_axis=0, concat_axis=0, tiled=T...  21.2 us
    pallas_call x1, Pallas kernels, inner_call(): pl.pallas_call(inner_kernel, in_specs=[hbm] * 7, out_specs=[hbm, hbm], ou...  9.88 us

profile of v9, /device:TPU:1, one launch (start us, length us, event | category | flops | bytes accessed | tf_op | source)
XLA Modules:
  0.0 115.0 jit_solution(8942497470778604709)
XLA Ops:
  0.6 9.9 %inner.1 = (bf16[256,512]{1,0:T(8,128)(2,1)}, bf16[16,16,2,896]{3,2,1,0:T(2,128)(2,1)}) custom-call(bf16[16,128,512]{2,1,0:T(8,128)(2,1)} %events_hbm.1, bf16[16,512]{1,0:T(8,128)(2,1)} %bitcast.9, bf16[512,1536]{1,0:T(8,128)(2,1)} %inner_qkv_hbm.1, bf16[512,512]{1,0:T(8,128)(2,1)} %inner_out_hbm.1, f32[1,512]{1,0:T(1,128)} %bitcast.10, f32[1,512]{1,0:T(1,128)} %bitcast.11, ...), custom_call_target="tpu_custom_call" | custom-call | tf_op jit(solution)/shard_map/inner/pallas_call | solution.py:250
  10.5 0.0 copy-start.2
  10.5 0.0 copy-start
  10.5 0.0 copy-start.1
  10.6 44.3 %all_to_all.10.recv_ref = bf16[256,2,896]{2,1,0:T(2,128)(2,1)S(1)} all-to-all(bf16[256,2,896]{2,1,0:T(2,128)(2,1)} %bitcast.7), channel_id=1, replica_groups=mesh['seq'=128,'head'=2] {'seq','head'}, dimensions={0} | all-to-all | bytes 1835008 | tf_op jit(solution)/shard_map/all_to_all | solution.py:475
  54.8 0.0 copy-done.2
  54.8 37.3 %attend.1 = (bf16[256,2,256]{2,1,0:T(2,128)(2,1)S(1)}, bf16[1,1,4096]{2,1,0:T(2,128)(2,1)}) custom-call(s32[16]{0:T(128)S(1)} %copy-done.2, bf16[256,2,896]{2,1,0:T(2,128)(2,1)S(1)} %all_to_all.10.recv_ref), custom_call_target="tpu_custom_call" | custom-call | tf_op jit(solution)/shard_map/attend/pallas_call | solution.py:396
  92.2 21.2 %all_to_all.11 = bf16[256,2,256]{2,1,0:T(2,128)(2,1)S(1)} all-to-all(bf16[256,2,256]{2,1,0:T(2,128)(2,1)S(1)} %get-tuple-element.7), channel_id=1, replica_groups=mesh['seq'=128,'head'=2] {'seq','head'}, dimensions={0} | all-to-all | bytes 524288 | tf_op jit(solution)/shard_map/all_to_all | solution.py:479
  113.3 0.0 copy-done
  113.3 0.0 copy-done.1
  113.3 1.7 %output.1 = bf16[256,512]{1,0:T(8,128)(2,1)} custom-call(bf16[16,16,2,256]{3,2,1,0:T(2,128)(2,1)S(1)} %bitcast.6, bf16[256,512]{1,0:T(8,128)(2,1)S(1)} %copy-done.1, bf16[512,512]{1,0:T(8,128)(2,1)S(1)} %copy-done), custom_call_target="tpu_custom_call" | custom-call | tf_op jit(solution)/shard_map/output/pallas_call | solution.py:441
Async XLA Ops:
  10.5 44.3 %copy-start.2 = (s32[16]{0:T(128)S(1)}, s32[16]{0:T(128)}, u32[]{:S(2)}) copy-start(s32[16]{0:T(128)} %lengths_ref.1) | copy-start | bytes 196
  10.5 102.8 %copy-start = (bf16[512,512]{1,0:T(8,128)(2,1)S(1)}, bf16[512,512]{1,0:T(8,128)(2,1)}, u32[]{:S(2)}) copy-start(bf16[512,512]{1,0:T(8,128)(2,1)} %mixed_out_ref.1) | copy-start | bytes 1572868
  10.5 102.8 %copy-start.1 = (bf16[256,512]{1,0:T(8,128)(2,1)S(1)}, bf16[256,512]{1,0:T(8,128)(2,1)}, u32[]{:S(2)}) copy-start(bf16[256,512]{1,0:T(8,128)(2,1)} %get-tuple-element.8.merged_ref) | copy-start | bytes 786436
